TPU v7x, 32 devices: a whole 2x2x4 slice. The times are simulated.
32 devices in a mesh: seg: 8 (over z, x), rep: 4 (over y, core).
Axes of the slice: x: 2, y: 2, z: 4, core: 2. Of those that a mesh axis runs over, the one named last changes fastest.
Arguments:
- layer_input: bfloat16 [4, 1536, 1024], P('rep', 'seg'), may hold values from -6 to 6
- live: int32 [4, 1536], P('rep', 'seg'), may hold values from 0 to 1, as said below
- knn_index: int32 [4, 1536, 128], P('rep', 'seg'), may hold values from -1 to 2879, as said below
- mem_keys: bfloat16 [4, 1536, 1024], P('rep', 'seg'), may hold values from -6 to 6
- mem_values: bfloat16 [4, 1536, 1024], P('rep', 'seg'), may hold values from -6 to 6
- gain_attn: bfloat16 [1024], P(('seg', 'rep')), may hold values from 0.099609375 to 1.8984375
- w_query: bfloat16 [1024, 1024], P(('seg', 'rep')), may hold values from -0.1875 to 0.1875
- w_key: bfloat16 [1024, 1024], P(('seg', 'rep')), may hold values from -0.1875 to 0.1875
- w_value: bfloat16 [1024, 1024], P(('seg', 'rep')), may hold values from -0.1875 to 0.1875
- w_out: bfloat16 [1024, 1024], P(('seg', 'rep')), may hold values from -2 to 2
- gain_ffn: bfloat16 [1024], P(('seg', 'rep')), may hold values from 0.099609375 to 1.8984375
- w_gate: bfloat16 [1024, 2816], P(('seg', 'rep')), may hold values from -0.1875 to 0.1875
- w_up: bfloat16 [1024, 2816], P(('seg', 'rep')), may hold values from -0.1875 to 0.1875
- w_down: bfloat16 [2816, 1024], P(('seg', 'rep')), may hold values from -0.109375 to 0.109375
- cotangent: bfloat16 [4, 1536, 1024], P('rep', 'seg'), may hold values from -6 to 6
Outputs:
- layer_output: bfloat16 [4, 1536, 1024], P('rep', 'seg')
- grad_x: bfloat16 [4, 1536, 1024], P('rep', 'seg')
- grad_gain_attn: float32 [1024], P(('seg', 'rep'))
- grad_w_query: float32 [1024, 1024], P(('seg', 'rep'))
- grad_w_key: float32 [1024, 1024], P(('seg', 'rep'))
- grad_w_value: float32 [1024, 1024], P(('seg', 'rep'))
- grad_w_out: float32 [1024, 1024], P(('seg', 'rep'))
- grad_gain_ffn: float32 [1024], P(('seg', 'rep'))
- grad_w_gate: float32 [1024, 2816], P(('seg', 'rep'))
- grad_w_up: float32 [1024, 2816], P(('seg', 'rep'))
- grad_w_down: float32 [2816, 1024], P(('seg', 'rep'))
Inputs may be any that keep to these rules, and one draw needn't show every extreme that they name: `knn_index`: each pick is a live slot of the query's row (m) or of the paired row (1536 + m) that lies in an earlier segment than the query's own; -1 marks an empty pick; a slot may repeat and counts once; queries of a row's first segment retrieve nothing. Padded slots fill the tail of a document's last segment; the first token of every segment is live; in every draw some pair of rows each hold one document over all their segments.
All inputs are finite; a program needn't handle non-finite values.
Results may differ from a plain program's by a relative error of at most 0.023.
Values may be sent and summed in bfloat16 or wider, within the bound.
No kernel may reach another device: no remote copies, remote signals or barrier semaphores. Data moves between devices by JAX's collectives and lax.ppermute only.
A program may use at most 320 MiB of HBM per device.

v0:
```python
import jax
import jax.numpy as jnp
from jax import lax
from jax.sharding import PartitionSpec as P

H = 8
HD = 128
MICRO = 4


EPSILON = 1e-05
NEG_BIG = -1e30
ROPE_BASE = 10000.0
BLOCK_ROWS = 512


def from_partner(block, axis, distance):
    count = lax.axis_size(axis)
    route = []
    for low in range(count):
        high = low | 1 << distance
        if high != low and high < count:
            route += [(low, high), (high, low)]
    return lax.ppermute(block, axis, route)


def norm_forward(values, gain):
    inverse = lax.rsqrt(jnp.mean(values * values, axis=-1, keepdims=True) + EPSILON)
    return (values * inverse * gain, inverse)


def norm_backward(values, inverse, gain, grad_out):
    normed = values * inverse
    grad_gain = jnp.sum(grad_out * normed, axis=0)
    scaled = grad_out * gain
    grad_values = inverse * (scaled - normed * jnp.mean(scaled * normed, axis=-1, keepdims=True))
    return (grad_values, grad_gain)


def rope_table(seg_len, head_dim):
    position = jnp.arange(seg_len).astype(jnp.float32)
    freqs = ROPE_BASE ** (-(2.0 * jnp.arange(head_dim // 2).astype(jnp.float32)) / head_dim)
    angle = position[:, None] * freqs[None, :]
    return (jnp.cos(angle), jnp.sin(angle))


def rotate(values, cosine, sine, sign):
    half = values.shape[-1] // 2
    first = values[..., :half]
    second = values[..., half:]
    cos_b = cosine[:, None, :]
    sin_b = sign * sine[:, None, :]
    return jnp.concatenate([first * cos_b - second * sin_b, first * sin_b + second * cos_b], -1)


def matmul(left, right):
    return jnp.dot(left, right, preferred_element_type=jnp.float32)


def matmul_rows(left, right):
    return lax.dot_general(
        left, right, (((0,), (0,)), ((), ())), preferred_element_type=jnp.float32
    )


def matmul_cols(left, right):
    return lax.dot_general(
        left, right, (((1,), (1,)), ((), ())), preferred_element_type=jnp.float32
    )


def blocked(step_fn, running, pieces):
    row_count = pieces[0].shape[0]
    n_blocks = row_count // BLOCK_ROWS
    stacked = tuple((piece.reshape((n_blocks, BLOCK_ROWS) + piece.shape[1:]) for piece in pieces))

    def one_block(state, item):
        block_pieces, block_no = item
        return (step_fn(state, block_pieces, block_no * BLOCK_ROWS), None)

    running, unused = lax.scan(one_block, running, (stacked, jnp.arange(n_blocks, dtype=jnp.int32)))
    return running


def fold_pieces(piece, groups):
    return jnp.sum(piece.reshape((groups, piece.shape[0] // groups) + piece.shape[1:]), axis=0)


def local(
    layer_input,
    live,
    knn_index,
    mem_keys,
    mem_values,
    gain_attn,
    w_query,
    w_key,
    w_value,
    w_out,
    gain_ffn,
    w_gate,
    w_up,
    w_down,
    cotangent,
):
    seg_len = layer_input.shape[1]
    width = layer_input.shape[2]
    heads = H
    head_dim = HD
    groups = lax.axis_size("seg")
    tokens = seg_len * groups
    scale = head_dim ** (-0.5)
    micro_len = seg_len // MICRO
    shards = (gain_attn, w_query, w_key, w_value, w_out, gain_ffn, w_gate, w_up, w_down)
    g_attn, wq, wk, wv, wo, g_ffn, wg, wu, wd = (
        lax.all_gather(shards[0], ("seg", "rep"), axis=0, tiled=True),
        lax.all_gather(shards[1], ("seg", "rep"), axis=0, tiled=True),
        lax.all_gather(shards[2], ("seg", "rep"), axis=0, tiled=True),
        lax.all_gather(shards[3], ("seg", "rep"), axis=0, tiled=True),
        lax.all_gather(shards[4], ("seg", "rep"), axis=0, tiled=True),
        lax.all_gather(shards[5], ("seg", "rep"), axis=0, tiled=True),
        lax.all_gather(shards[6], ("seg", "rep"), axis=0, tiled=True),
        lax.all_gather(shards[7], ("seg", "rep"), axis=0, tiled=True),
        lax.all_gather(shards[8], ("seg", "rep"), axis=0, tiled=True),
    )
    own_keys = mem_keys[0]
    own_values = mem_values[0]
    pair_keys, pair_values = from_partner((own_keys, own_values), "rep", 0)
    cache_pieces = (own_keys, own_values, pair_keys, pair_values)
    x_float = layer_input[0].astype(jnp.float32)
    cosine, sine = rope_table(seg_len, head_dim)
    h_float, inv_one = norm_forward(x_float, g_attn.astype(jnp.float32))
    h_one = h_float.astype(jnp.bfloat16)
    queries = rotate(matmul(h_one, wq).reshape(seg_len, heads, head_dim), cosine, sine, 1.0).astype(
        jnp.bfloat16
    )
    keys_local = rotate(
        matmul(h_one, wk).reshape(seg_len, heads, head_dim), cosine, sine, 1.0
    ).astype(jnp.bfloat16)
    values_local = matmul(h_one, wv).astype(jnp.bfloat16).reshape(seg_len, heads, head_dim)
    position = jnp.arange(seg_len, dtype=jnp.int32)
    allow_local = (position[None, :] <= position[:, None]) & (
        (live[0][None, :] == 1) | (position[None, :] == position[:, None])
    )
    columns = jnp.where(knn_index[0] >= 0, knn_index[0], 2 * tokens)
    allow_mem = (
        jnp.zeros((seg_len, 2 * tokens), jnp.bfloat16)
        .at[position[:, None], columns]
        .set(1.0, mode="drop")
    )

    def local_scores(row_lo, row_hi):
        scores = (
            jnp.einsum(
                "qhd,khd->hqk",
                queries[row_lo:row_hi],
                keys_local[:row_hi],
                preferred_element_type=jnp.float32,
            )
            * scale
        )
        return jnp.where(allow_local[row_lo:row_hi, :row_hi][None], scores, NEG_BIG)

    def memory_scores(keys_piece, first_col):
        row_count = keys_piece.shape[0]
        scores = (
            jnp.einsum(
                "qhd,khd->hqk",
                queries,
                keys_piece.reshape(row_count, heads, head_dim),
                preferred_element_type=jnp.float32,
            )
            * scale
        )
        allowed = lax.dynamic_slice_in_dim(allow_mem, first_col, row_count, 1)
        return jnp.where(allowed[None] > 0, scores, NEG_BIG)

    max_parts = []
    total_parts = []
    acc_parts = []
    for micro_no in range(MICRO):
        row_lo = micro_no * micro_len
        row_hi = row_lo + micro_len
        scores = local_scores(row_lo, row_hi)
        row_max = jnp.max(scores, axis=-1)
        expo = jnp.exp(scores - row_max[..., None])
        max_parts.append(row_max)
        total_parts.append(jnp.sum(expo, axis=-1))
        acc_parts.append(
            jnp.einsum(
                "hqk,khd->hqd",
                expo.astype(jnp.bfloat16),
                values_local[:row_hi],
                preferred_element_type=jnp.float32,
            )
        )
    start_state = (
        jnp.concatenate(max_parts, 1),
        jnp.concatenate(total_parts, 1),
        jnp.concatenate(acc_parts, 1),
    )

    def memory_pair(running, keys_piece, values_piece, first_col):
        row_max, row_total, acc_out = running
        row_count = keys_piece.shape[0]
        scores = memory_scores(keys_piece, first_col)
        new_max = jnp.maximum(row_max, jnp.max(scores, axis=-1))
        shrink = jnp.exp(row_max - new_max)
        expo = jnp.exp(scores - new_max[..., None])
        row_total = row_total * shrink + jnp.sum(expo, axis=-1)
        acc_out = acc_out * shrink[..., None] + jnp.einsum(
            "hqk,khd->hqd",
            expo.astype(jnp.bfloat16),
            values_piece.reshape(row_count, heads, head_dim),
            preferred_element_type=jnp.float32,
        )
        return (new_max, row_total, acc_out)

    def memory_step(running, pieces, first_row):
        running = memory_pair(running, pieces[0], pieces[1], first_row)
        return memory_pair(running, pieces[2], pieces[3], first_row + tokens)

    row_max, row_total, acc_out = blocked(
        memory_step,
        start_state,
        (
            lax.all_gather(cache_pieces[0], "seg", axis=0, tiled=True),
            lax.all_gather(cache_pieces[1], "seg", axis=0, tiled=True),
            lax.all_gather(cache_pieces[2], "seg", axis=0, tiled=True),
            lax.all_gather(cache_pieces[3], "seg", axis=0, tiled=True),
        ),
    )
    log_total = row_max + jnp.log(row_total)
    attn_heads = acc_out / row_total[..., None]
    attended = attn_heads.transpose(1, 0, 2).reshape(seg_len, width).astype(jnp.bfloat16)
    x_one = x_float + matmul(attended, wo)
    g_ffn_f = g_ffn.astype(jnp.float32)
    h_two_f, inv_two = norm_forward(x_one, g_ffn_f)
    h_two = h_two_f.astype(jnp.bfloat16)
    gate = matmul(h_two, wg)
    upward = matmul(h_two, wu)
    sigma = jax.nn.sigmoid(gate)
    swish = gate * sigma
    hidden = (swish * upward).astype(jnp.bfloat16)
    layer_output = (x_one + matmul(hidden, wd)).astype(jnp.bfloat16)
    g_attn, wq, wk, wv, wo, g_ffn, wg, wu, wd = (
        lax.all_gather(shards[0], ("seg", "rep"), axis=0, tiled=True),
        lax.all_gather(shards[1], ("seg", "rep"), axis=0, tiled=True),
        lax.all_gather(shards[2], ("seg", "rep"), axis=0, tiled=True),
        lax.all_gather(shards[3], ("seg", "rep"), axis=0, tiled=True),
        lax.all_gather(shards[4], ("seg", "rep"), axis=0, tiled=True),
        lax.all_gather(shards[5], ("seg", "rep"), axis=0, tiled=True),
        lax.all_gather(shards[6], ("seg", "rep"), axis=0, tiled=True),
        lax.all_gather(shards[7], ("seg", "rep"), axis=0, tiled=True),
        lax.all_gather(shards[8], ("seg", "rep"), axis=0, tiled=True),
    )
    grad_out = cotangent[0]
    grad_wd = matmul_rows(hidden, grad_out)
    d_hidden = matmul_cols(grad_out, wd)
    d_gate = (d_hidden * upward * sigma * (1.0 + gate * (1.0 - sigma))).astype(jnp.bfloat16)
    d_up = (d_hidden * swish).astype(jnp.bfloat16)
    grad_wg = matmul_rows(h_two, d_gate)
    grad_wu = matmul_rows(h_two, d_up)
    d_h_two = matmul_cols(d_gate, wg) + matmul_cols(d_up, wu)
    d_x_norm, grad_g_ffn = norm_backward(x_one, inv_two, g_ffn.astype(jnp.float32), d_h_two)
    d_x_one = grad_out.astype(jnp.float32) + d_x_norm
    d_branch = d_x_one.astype(jnp.bfloat16)
    grad_wo = matmul_rows(attended, d_branch)
    d_attended = matmul_cols(d_branch, wo).astype(jnp.bfloat16)
    d_heads = d_attended.reshape(seg_len, heads, head_dim).transpose(1, 0, 2)
    delta = jnp.sum(d_heads.astype(jnp.float32) * attn_heads, axis=-1)
    dq_parts = []
    d_keys = jnp.zeros((seg_len, heads, head_dim), jnp.float32)
    d_values = jnp.zeros((seg_len, heads, head_dim), jnp.float32)
    for micro_no in range(MICRO):
        row_lo = micro_no * micro_len
        row_hi = row_lo + micro_len
        chances = jnp.exp(local_scores(row_lo, row_hi) - log_total[:, row_lo:row_hi, None])
        d_chances = jnp.einsum(
            "hqd,khd->hqk",
            d_heads[:, row_lo:row_hi],
            values_local[:row_hi],
            preferred_element_type=jnp.float32,
        )
        d_scores = (chances * (d_chances - delta[:, row_lo:row_hi, None])).astype(jnp.bfloat16)
        dq_parts.append(
            scale
            * jnp.einsum(
                "hqk,khd->hqd", d_scores, keys_local[:row_hi], preferred_element_type=jnp.float32
            )
        )
        d_keys = d_keys.at[:row_hi].add(
            scale
            * jnp.einsum(
                "hqk,qhd->khd", d_scores, queries[row_lo:row_hi], preferred_element_type=jnp.float32
            )
        )
        d_values = d_values.at[:row_hi].add(
            jnp.einsum(
                "hqk,hqd->khd",
                chances.astype(jnp.bfloat16),
                d_heads[:, row_lo:row_hi],
                preferred_element_type=jnp.float32,
            )
        )
    dq_local = jnp.concatenate(dq_parts, 1)

    def grad_pair(running, keys_piece, values_piece, first_col):
        row_count = keys_piece.shape[0]
        chances = jnp.exp(memory_scores(keys_piece, first_col) - log_total[..., None])
        d_chances = jnp.einsum(
            "hqd,khd->hqk",
            d_heads,
            values_piece.reshape(row_count, heads, head_dim),
            preferred_element_type=jnp.float32,
        )
        d_scores = (chances * (d_chances - delta[..., None])).astype(jnp.bfloat16)
        return running + scale * jnp.einsum(
            "hqk,khd->hqd",
            d_scores,
            keys_piece.reshape(row_count, heads, head_dim),
            preferred_element_type=jnp.float32,
        )

    def memory_grad(running, pieces, first_row):
        running = grad_pair(running, pieces[0], pieces[1], first_row)
        return grad_pair(running, pieces[2], pieces[3], first_row + tokens)

    d_queries = blocked(
        memory_grad,
        dq_local,
        (
            lax.all_gather(cache_pieces[0], "seg", axis=0, tiled=True),
            lax.all_gather(cache_pieces[1], "seg", axis=0, tiled=True),
            lax.all_gather(cache_pieces[2], "seg", axis=0, tiled=True),
            lax.all_gather(cache_pieces[3], "seg", axis=0, tiled=True),
        ),
    )
    dq_low = (
        rotate(d_queries.transpose(1, 0, 2), cosine, sine, -1.0)
        .reshape(seg_len, width)
        .astype(jnp.bfloat16)
    )
    dk_low = rotate(d_keys, cosine, sine, -1.0).reshape(seg_len, width).astype(jnp.bfloat16)
    dv_low = d_values.reshape(seg_len, width).astype(jnp.bfloat16)
    grad_wq = matmul_rows(h_one, dq_low)
    grad_wk = matmul_rows(h_one, dk_low)
    grad_wv = matmul_rows(h_one, dv_low)
    d_h_one = matmul_cols(dq_low, wq) + matmul_cols(dk_low, wk) + matmul_cols(dv_low, wv)
    d_x_first, grad_g_attn = norm_backward(x_float, inv_one, g_attn.astype(jnp.float32), d_h_one)
    grad_x = (d_x_one + d_x_first).astype(jnp.bfloat16)
    received = (
        lax.all_to_all(
            grad_g_attn.astype(jnp.bfloat16), "seg", split_axis=0, concat_axis=0, tiled=True
        ).astype(grad_g_attn.dtype),
        lax.all_to_all(
            grad_wq.astype(jnp.bfloat16), "seg", split_axis=0, concat_axis=0, tiled=True
        ).astype(grad_wq.dtype),
        lax.all_to_all(
            grad_wk.astype(jnp.bfloat16), "seg", split_axis=0, concat_axis=0, tiled=True
        ).astype(grad_wk.dtype),
        lax.all_to_all(
            grad_wv.astype(jnp.bfloat16), "seg", split_axis=0, concat_axis=0, tiled=True
        ).astype(grad_wv.dtype),
        lax.all_to_all(
            grad_wo.astype(jnp.bfloat16), "seg", split_axis=0, concat_axis=0, tiled=True
        ).astype(grad_wo.dtype),
        lax.all_to_all(
            grad_g_ffn.astype(jnp.bfloat16), "seg", split_axis=0, concat_axis=0, tiled=True
        ).astype(grad_g_ffn.dtype),
        lax.all_to_all(
            grad_wg.astype(jnp.bfloat16), "seg", split_axis=0, concat_axis=0, tiled=True
        ).astype(grad_wg.dtype),
        lax.all_to_all(
            grad_wu.astype(jnp.bfloat16), "seg", split_axis=0, concat_axis=0, tiled=True
        ).astype(grad_wu.dtype),
        lax.all_to_all(
            grad_wd.astype(jnp.bfloat16), "seg", split_axis=0, concat_axis=0, tiled=True
        ).astype(grad_wd.dtype),
    )
    g0, g1, g2, g3, g4, g5, g6, g7, g8 = received
    partial_sums = (
        fold_pieces(g0, groups),
        fold_pieces(g1, groups),
        fold_pieces(g2, groups),
        fold_pieces(g3, groups),
        fold_pieces(g4, groups),
        fold_pieces(g5, groups),
        fold_pieces(g6, groups),
        fold_pieces(g7, groups),
        fold_pieces(g8, groups),
    )
    summed = (
        lax.psum_scatter(
            partial_sums[0].astype(jnp.bfloat16), "rep", scatter_dimension=0, tiled=True
        ).astype(jnp.float32),
        lax.psum_scatter(
            partial_sums[1].astype(jnp.bfloat16), "rep", scatter_dimension=0, tiled=True
        ).astype(jnp.float32),
        lax.psum_scatter(
            partial_sums[2].astype(jnp.bfloat16), "rep", scatter_dimension=0, tiled=True
        ).astype(jnp.float32),
        lax.psum_scatter(
            partial_sums[3].astype(jnp.bfloat16), "rep", scatter_dimension=0, tiled=True
        ).astype(jnp.float32),
        lax.psum_scatter(
            partial_sums[4].astype(jnp.bfloat16), "rep", scatter_dimension=0, tiled=True
        ).astype(jnp.float32),
        lax.psum_scatter(
            partial_sums[5].astype(jnp.bfloat16), "rep", scatter_dimension=0, tiled=True
        ).astype(jnp.float32),
        lax.psum_scatter(
            partial_sums[6].astype(jnp.bfloat16), "rep", scatter_dimension=0, tiled=True
        ).astype(jnp.float32),
        lax.psum_scatter(
            partial_sums[7].astype(jnp.bfloat16), "rep", scatter_dimension=0, tiled=True
        ).astype(jnp.float32),
        lax.psum_scatter(
            partial_sums[8].astype(jnp.bfloat16), "rep", scatter_dimension=0, tiled=True
        ).astype(jnp.float32),
    )
    return (
        layer_output[None],
        grad_x[None],
        summed[0],
        summed[1],
        summed[2],
        summed[3],
        summed[4],
        summed[5],
        summed[6],
        summed[7],
        summed[8],
    )


def solution(mesh):
    return jax.shard_map(
        local,
        mesh=mesh,
        in_specs=(
            P("rep", "seg", None),
            P("rep", "seg"),
            P("rep", "seg", None),
            P("rep", "seg", None),
            P("rep", "seg", None),
            P(("seg", "rep")),
            P(("seg", "rep"), None),
            P(("seg", "rep"), None),
            P(("seg", "rep"), None),
            P(("seg", "rep"), None),
            P(("seg", "rep")),
            P(("seg", "rep"), None),
            P(("seg", "rep"), None),
            P(("seg", "rep"), None),
            P("rep", "seg", None),
        ),
        out_specs=(
            P("rep", "seg", None),
            P("rep", "seg", None),
            P(("seg", "rep")),
            P(("seg", "rep"), None),
            P(("seg", "rep"), None),
            P(("seg", "rep"), None),
            P(("seg", "rep"), None),
            P(("seg", "rep")),
            P(("seg", "rep"), None),
            P(("seg", "rep"), None),
            P(("seg", "rep"), None),
        ),
        check_vma=False,
    )
```

profile of v0, /device:TPU:0, one launch (start us, length us, event | category | flops | bytes accessed | tf_op | source)
XLA Modules:
  0.0 1445.6 jit_solution(2338434266941190921)
XLA Ops:
  21.9 42.0 %all-reduce.6 = (bf16[1024]{0:T(1024)(128)(2,1)S(1)}, bf16[1024]{0:T(1024)(128)(2,1)S(1)}) all-reduce(bf16[1024]{0:T(1024)(128)(2,1)S(1)} %dynamic-update-slice.22, bf16[1024]{0:T(1024)(128)(2,1)S(1)} %dynamic-update-slice.23), channel_id=1, replica_groups=mesh['seg'=8,'rep'=4] {'seg','rep'}, use_global_device_ids=true, to_apply=%add.2 | all-reduce | flops 2048 | bytes 8192
  65.7 169.0 %scatter_custom_fusion = bf16[589824]{0:T(1024)(128)(2,1)S(1)} fusion(s32[24576]{0:T(1024)S(1)} %select_bitcast_fusion, bf16[24576]{0:T(1024)(128)(2,1)S(1)} %broadcast.454, bf16[]{:T(256)} %constant.371.clone.1), kind=kCustom, calls=%fused_computation.167 | custom fusion | bytes 1179650
  259.2 50.1 %all-gather.34.cloned.1.call-done = bf16[1,1536,1024]{2,1,0:T(8,128)(2,1)} async-done(((bf16[1,192,1024]{2,1,0:T(8,128)(2,1)}), bf16[1,1536,1024]{2,1,0:T(8,128)(2,1)}) %all-gather.34.cloned.1.call-update) | async-done | bytes 3145744 | tf_op jit(solution)/shard_map/all_gather | solution.py:228
  314.0 57.0 %all-gather.20.cloned.1.call-done = bf16[1536,1024]{1,0:T(8,128)(2,1)} async-done(((bf16[192,1024]{1,0:T(8,128)(2,1)}), bf16[1536,1024]{1,0:T(8,128)(2,1)}) %all-gather.20.cloned.1.call-update) | async-done | bytes 3145744 | tf_op jit(solution)/shard_map/all_gather | solution.py:229
  375.7 57.2 %all-gather.22.cloned.1.call-done = bf16[1536,1024]{1,0:T(8,128)(2,1)} async-done(((bf16[192,1024]{1,0:T(8,128)(2,1)}), bf16[1536,1024]{1,0:T(8,128)(2,1)}) %all-gather.22.cloned.1.call-update) | async-done | bytes 3145744 | tf_op jit(solution)/shard_map/all_gather | solution.py:230
  437.6 39.0 %while.38 = (s32[]{:T(128)}, f32[8,192]{1,0:T(8,128)S(1)}, f32[8,192]{1,0:T(8,128)S(1)}, f32[8,192,128]{2,1,0:T(8,128)}, s32[3]{0:T(128)S(1)}, /*index=5*/bf16[1...) while((s32[]{:T(128)}, f32[8,192]{1,0:T(8,128)S(1)}, ...), condition=%wide.region_15.16_spmd, body=%wide.region_10.15_spmd.sunk | while | flops 823891968 | bytes 39874872 | solution.py:81
  476.5 14.3 all-gather.24.cloned.1.call-done
  494.4 65.4 %all-gather.26.cloned.1.call-done = bf16[1024,2816]{1,0:T(8,128)(2,1)} async-done(((bf16[32,2816]{1,0:T(8,128)(2,1)}), bf16[1024,2816]{1,0:T(8,128)(2,1)}) %all-gather.26.cloned.1.call-update) | async-done | bytes 5767184 | tf_op jit(solution)/shard_map/all_gather | solution.py:122
  565.1 63.8 %all-gather.28.cloned.1.call-done = bf16[1024,2816]{1,0:T(8,128)(2,1)} async-done(((bf16[32,2816]{1,0:T(8,128)(2,1)}), bf16[1024,2816]{1,0:T(8,128)(2,1)}) %all-gather.28.cloned.1.call-update) | async-done | bytes 5767184 | tf_op jit(solution)/shard_map/all_gather | solution.py:123
  634.1 63.9 %all-gather.30.cloned.1.call-done = bf16[2816,1024]{1,0:T(8,128)(2,1)} async-done(((bf16[88,1024]{1,0:T(8,128)(2,1)}), bf16[2816,1024]{1,0:T(8,128)(2,1)}) %all-gather.30.cloned.1.call-update) | async-done | bytes 5767184 | tf_op jit(solution)/shard_map/all_gather | solution.py:124
  698.0 7.4 multiply_convert_fusion
  705.5 5.5 fusion.222
  720.8 60.9 %while.39 = (s32[]{:T(128)}, f32[8,192,128]{2,1,0:T(8,128)}, s32[3]{0:T(128)S(1)}, bf16[192,3072]{1,0:T(8,128)(2,1)}, bf16[3,512,1024]{1,2,0:T(8,128)(2,1)}, /*i...) while((s32[]{:T(128)}, f32[8,192,128]{2,1,0:T(8,128)}, ...), condition=%wide.region_20.21_spmd, body=%wide.region_19.20_spmd.sunk | while | flops 1218674688 | bytes 32792868 | solution.py:81
  795.7 45.5 %all-to-all-done.1 = bf16[8,128,1024]{2,1,0:T(8,128)(2,1)S(1)} async-done(((bf16[8,128,1024]{2,1,0:T(8,128)(2,1)}), bf16[8,128,1024]{2,1,0:T(8,128)(2,1)S(1)}, u32[]{:S(2)}, u32[]{:S(2)}) %all-to-all-start.1) | async-done | bytes 2097184 | tf_op jit(solution)/shard_map/all_to_all | solution.py:356
  853.2 40.3 %all-to-all-done.2 = bf16[8,128,1024]{2,1,0:T(8,128)(2,1)} async-done(((bf16[8,128,1024]{2,1,0:T(8,128)(2,1)}), bf16[8,128,1024]{2,1,0:T(8,128)(2,1)}, u32[]{:S(2)}, u32[]{:S(2)}) %all-to-all-start.2) | async-done | bytes 2097184 | tf_op jit(solution)/shard_map/all_to_all | solution.py:359
  901.9 43.7 %all-to-all-done.3 = bf16[8,128,1024]{2,1,0:T(8,128)(2,1)} async-done(((bf16[8,128,1024]{2,1,0:T(8,128)(2,1)}), bf16[8,128,1024]{2,1,0:T(8,128)(2,1)}, u32[]{:S(2)}, u32[]{:S(2)}) %all-to-all-start.3) | async-done | bytes 2097184 | tf_op jit(solution)/shard_map/all_to_all | solution.py:362
  950.0 5.5 convolution_convert_fusion.2
  955.4 42.3 %all-to-all-done.4 = bf16[8,128,1024]{2,1,0:T(8,128)(2,1)} async-done(((bf16[8,128,1024]{2,1,0:T(8,128)(2,1)}), bf16[8,128,1024]{2,1,0:T(8,128)(2,1)}, u32[]{:S(2)}, u32[]{:S(2)}) %all-to-all-start.4) | async-done | bytes 2097184 | tf_op jit(solution)/shard_map/all_to_all | solution.py:365
  1002.7 5.5 convolution_convert_fusion.1
  1008.1 120.4 %all-to-all-done.6 = bf16[8,128,2816]{2,1,0:T(8,128)(2,1)} async-done(((bf16[8,128,2816]{2,1,0:T(8,128)(2,1)}), bf16[8,128,2816]{2,1,0:T(8,128)(2,1)}, u32[]{:S(2)}, u32[]{:S(2)}) %all-to-all-start.6) | async-done | bytes 5767200 | tf_op jit(solution)/shard_map/all_to_all | solution.py:371
  1133.4 5.4 convolution_convert_fusion
  1138.9 120.6 %all-to-all-done.7 = bf16[8,128,2816]{2,1,0:T(8,128)(2,1)} async-done(((bf16[8,128,2816]{2,1,0:T(8,128)(2,1)}), bf16[8,128,2816]{2,1,0:T(8,128)(2,1)}, u32[]{:S(2)}, u32[]{:S(2)}) %all-to-all-start.7) | async-done | bytes 5767200 | tf_op jit(solution)/shard_map/all_to_all | solution.py:374
  1288.5 101.8 %all-to-all-done.8 = bf16[8,352,1024]{2,1,0:T(8,128)(2,1)} async-done(((bf16[8,352,1024]{2,1,0:T(8,128)(2,1)}), bf16[8,352,1024]{2,1,0:T(8,128)(2,1)}, u32[]{:S(2)}, u32[]{:S(2)}) %all-to-all-start.8) | async-done | bytes 5767200 | tf_op jit(solution)/shard_map/all_to_all | solution.py:377
  1420.6 5.7 all-reduce.7
  (333 shorter events, 292.4 us)
Async XLA Ops:
  7.2 230.0 %all-gather.14.cloned.1.call-start = ((), (), s32[]{:S(2)}) async-start(), calls=%async_computation.16 | async-start | bytes 2162688 | tf_op jit(solution)/shard_map/all_gather | solution.py:117
  7.9 232.2 %all-gather.16.cloned.1.call-start = ((), (), s32[]{:S(2)}) async-start(), calls=%async_computation.17 | async-start | bytes 2162688 | tf_op jit(solution)/shard_map/all_gather | solution.py:118
  8.7 239.9 %all-gather.18.cloned.1.call-start = ((), (), s32[]{:S(2)}) async-start(), calls=%async_computation.18 | async-start | bytes 2162688 | tf_op jit(solution)/shard_map/all_gather | solution.py:119
  9.4 245.1 %all-gather.32.cloned.1.call-start = ((), (), s32[]{:S(2)}) async-start(), calls=%async_computation.32 | async-start | bytes 3538944 | tf_op jit(solution)/shard_map/all_gather | solution.py:227
  10.0 299.3 %all-gather.34.cloned.1.call-start = ((), (), s32[]{:S(2)}) async-start(), calls=%async_computation.33 | async-start | bytes 3538944 | tf_op jit(solution)/shard_map/all_gather | solution.py:228
  10.6 360.4 %all-gather.20.cloned.1.call-start = ((), (), s32[]{:S(2)}) async-start(), calls=%async_computation.19 | async-start | bytes 3538944 | tf_op jit(solution)/shard_map/all_gather | solution.py:229
  13.5 419.4 %all-gather.22.cloned.1.call-start = ((), (), s32[]{:S(2)}) async-start(), calls=%async_computation.20 | async-start | bytes 3538944 | tf_op jit(solution)/shard_map/all_gather | solution.py:230
  16.3 474.5 %all-gather.24.cloned.1.call-start = ((), (), s32[]{:S(2)}) async-start(), calls=%async_computation.21 | async-start | bytes 2162688 | tf_op jit(solution)/shard_map/all_gather | solution.py:120
  17.1 542.8 %all-gather.26.cloned.1.call-start = ((), (), s32[]{:S(2)}) async-start(), calls=%async_computation.22 | async-start | bytes 5947392 | tf_op jit(solution)/shard_map/all_gather | solution.py:122
  17.8 611.1 %all-gather.28.cloned.1.call-start = ((), (), s32[]{:S(2)}) async-start(), calls=%async_computation.23 | async-start | bytes 5947392 | tf_op jit(solution)/shard_map/all_gather | solution.py:123
  18.4 679.6 %all-gather.30.cloned.1.call-start = ((), (), s32[]{:S(2)}) async-start(), calls=%async_computation.24 | async-start | bytes 5947392 | tf_op jit(solution)/shard_map/all_gather | solution.py:124
  788.2 52.9 %all-to-all-start.1 = ((bf16[8,128,1024]{2,1,0:T(8,128)(2,1)}), bf16[8,128,1024]{2,1,0:T(8,128)(2,1)S(1)}, u32[]{:S(2)}, u32[]{:S(2)}) async-start(bf16[8,128,1024]{2,1,0:T(8,128)(2,1)} %bitcast.435), calls=%async_computation.1 | async-start | bytes 4194304 | tf_op jit(solution)/shard_map/all_to_all | solution.py:356
  841.1 52.3 %all-to-all-start.2 = ((bf16[8,128,1024]{2,1,0:T(8,128)(2,1)}), bf16[8,128,1024]{2,1,0:T(8,128)(2,1)}, u32[]{:S(2)}, u32[]{:S(2)}) async-start(bf16[8,128,1024]{2,1,0:T(8,128)(2,1)} %bitcast.433), calls=%async_computation.3 | async-start | bytes 4194304 | tf_op jit(solution)/shard_map/all_to_all | solution.py:359
  945.6 52.2 %all-to-all-start.4 = ((bf16[8,128,1024]{2,1,0:T(8,128)(2,1)}), bf16[8,128,1024]{2,1,0:T(8,128)(2,1)}, u32[]{:S(2)}, u32[]{:S(2)}) async-start(bf16[8,128,1024]{2,1,0:T(8,128)(2,1)} %bitcast.443), calls=%async_computation.7 | async-start | bytes 4194304 | tf_op jit(solution)/shard_map/all_to_all | solution.py:365
  997.8 130.8 %all-to-all-start.6 = ((bf16[8,128,2816]{2,1,0:T(8,128)(2,1)}), bf16[8,128,2816]{2,1,0:T(8,128)(2,1)}, u32[]{:S(2)}, u32[]{:S(2)}) async-start(bf16[8,128,2816]{2,1,0:T(8,128)(2,1)} %bitcast.425), calls=%async_computation.10 | async-start | bytes 11534336 | tf_op jit(solution)/shard_map/all_to_all | solution.py:371
  1128.6 130.9 %all-to-all-start.7 = ((bf16[8,128,2816]{2,1,0:T(8,128)(2,1)}), bf16[8,128,2816]{2,1,0:T(8,128)(2,1)}, u32[]{:S(2)}, u32[]{:S(2)}) async-start(bf16[8,128,2816]{2,1,0:T(8,128)(2,1)} %bitcast.426), calls=%async_computation.12 | async-start | bytes 11534336 | tf_op jit(solution)/shard_map/all_to_all | solution.py:374
  1259.5 130.8 %all-to-all-start.8 = ((bf16[8,352,1024]{2,1,0:T(8,128)(2,1)}), bf16[8,352,1024]{2,1,0:T(8,128)(2,1)}, u32[]{:S(2)}, u32[]{:S(2)}) async-start(bf16[8,352,1024]{2,1,0:T(8,128)(2,1)} %bitcast.424), calls=%async_computation.14 | async-start | bytes 11534336 | tf_op jit(solution)/shard_map/all_to_all | solution.py:377
  1264.2 163.3 %reduce-scatter.8.cloned.1.call-start = ((), (), s32[]{:S(2)}) async-start(), calls=%async_computation.25 | async-start | bytes 327680 | tf_op jit(solution)/shard_map/reduce_scatter | solution.py:397
  1265.4 163.6 %reduce-scatter.10.cloned.1.call-start = ((), (), s32[]{:S(2)}) async-start(), calls=%async_computation.26 | async-start | bytes 327680 | tf_op jit(solution)/shard_map/reduce_scatter | solution.py:400
  1268.2 162.3 %reduce-scatter.12.cloned.1.call-start = ((), (), s32[]{:S(2)}) async-start(), calls=%async_computation.27 | async-start | bytes 327680 | tf_op jit(solution)/shard_map/reduce_scatter | solution.py:403
  1271.0 161.0 %reduce-scatter.14.cloned.1.call-start = ((), (), s32[]{:S(2)}) async-start(), calls=%async_computation.28 | async-start | bytes 327680 | tf_op jit(solution)/shard_map/reduce_scatter | solution.py:406
  1273.8 159.7 %reduce-scatter.16.cloned.1.call-start = ((), (), s32[]{:S(2)}) async-start(), calls=%async_computation.29 | async-start | bytes 901120 | tf_op jit(solution)/shard_map/reduce_scatter | solution.py:412
  1278.5 156.7 %reduce-scatter.18.cloned.1.call-start = ((), (), s32[]{:S(2)}) async-start(), calls=%async_computation.30 | async-start | bytes 901120 | tf_op jit(solution)/shard_map/reduce_scatter | solution.py:415
  1283.2 153.6 %reduce-scatter.20.cloned.1.call-start = ((), (), s32[]{:S(2)}) async-start(), calls=%async_computation.31 | async-start | bytes 901120 | tf_op jit(solution)/shard_map/reduce_scatter | solution.py:418
  (49 other events, 675.3 us)
Sparse Core Ops, SparseCore 0:
  10.9 59.4 all-gather.13
  73.2 55.3 all-gather.15
  131.5 55.2 all-gather.17
  188.8 59.2 all-gather.31
  250.2 59.0 all-gather.33
  311.9 59.0 all-gather.19
  373.8 59.0 all-gather.21
  435.7 55.0 all-gather.23
  493.7 66.1 all-gather.25
  562.6 66.2 all-gather.27
  631.7 66.2 all-gather.29
  1267.7 21.1 reduce-scatter.7
  1292.1 20.0 reduce-scatter.9
  1315.1 20.0 reduce-scatter.11
  1337.6 20.0 reduce-scatter.13
  1360.1 22.8 reduce-scatter.15
  1385.5 22.8 reduce-scatter.17
  1410.8 22.8 reduce-scatter.19
where the time goes:
time: 1450 us
  waiting for transfers between devices  901 us (62%)
  local copies, waits for them, and re-layouts  228 us (16%)
  matrix products  141 us (10%)
  other arithmetic  64.1 us (4%)
  blocking collectives  47.7 us (3%)
  starting transfers between devices  42.4 us (3%)
  between operations  16.2 us (1%)
    unnamed x89, local copies, waits for them, and re-layouts  175 us
    all_to_all x1, waiting for transfers between devices, local(): lax.all_to_all(grad_wu.astype(jnp.bfloat16), 'seg', split_axis=0, concat_...  121 us
    all_to_all x1, waiting for transfers between devices, local(): lax.all_to_all(grad_wg.astype(jnp.bfloat16), 'seg', split_axis=0, concat_...  120 us
    all_to_all x1, waiting for transfers between devices, local(): lax.all_to_all(grad_wd.astype(jnp.bfloat16), 'seg', split_axis=0, concat_...  102 us
    all_gather x1, waiting for transfers between devices, local(): lax.all_gather(shards[6], ('seg', 'rep'), axis=0, tiled=True)  65.4 us
    all_gather x1, waiting for transfers between devices, local(): lax.all_gather(shards[8], ('seg', 'rep'), axis=0, tiled=True)  63.9 us
    all_gather x1, waiting for transfers between devices, local(): lax.all_gather(shards[7], ('seg', 'rep'), axis=0, tiled=True)  63.8 us
    all_gather x1, waiting for transfers between devices, local(): lax.all_gather(cache_pieces[3], 'seg', axis=0, tiled=True)  57.2 us
  transfers between devices with their start and end apart: 29, of which 18 were waited for; matrix products, arithmetic and copies ran while one was open for 24% of the time, Pallas kernels for 0%

commit v1 on v0

v1 whole, which is shorter than its diff:
```python
import jax
import jax.numpy as jnp
from jax import lax
from jax.experimental import pallas as pl
from jax.experimental.pallas import tpu as pltpu
from jax.sharding import PartitionSpec as P

H = 8
HD = 128
EPSILON = 1e-05
NEG_BIG = -1e30
POS_BIG = 1e30
ROPE_BASE = 10000.0
LANES = 128
KERNEL_SEGMENTS = 16

BF = jnp.bfloat16
F32 = jnp.float32


def cdiv(a, b):
    return -(-a // b)


def flip(value, axis, bit):
    count = lax.axis_size(axis)
    return lax.ppermute(value, axis, [(i, i ^ bit) for i in range(count)])


def core_swap(value):
    return flip(value, "rep", 1)


def ordered(mine, other, bit, axis):
    first = jnp.where(bit == 0, mine, other)
    second = jnp.where(bit == 0, other, mine)
    return jnp.concatenate([first, second], axis)


def pick(value, index, axis):
    return lax.dynamic_index_in_dim(value, index, axis, keepdims=False)


def seg_bits():
    bit = 2
    out = []
    while bit < lax.axis_size("seg"):
        out.append(bit)
        bit *= 2
    return out


def gather_chips(shard):
    rows, cols = shard.shape
    seg = lax.axis_index("seg")
    cur = shard[None, None]
    for bit in seg_bits():
        side = (seg // bit) % 2
        cur = ordered(cur, flip(cur, "seg", bit), side, 0)
    cur = cur.reshape(-1, 1, 1, rows, cols)
    cur = ordered(cur, flip(cur, "seg", 1), seg % 2, 1)
    cur = ordered(cur, flip(cur, "rep", 2), lax.axis_index("rep") // 2, 2)
    return cur.reshape(-1, cols)


def halve(value, axis_name, bit, side, axis):
    recv = flip(pick(value, 1 - side, axis), axis_name, bit)
    kept = pick(value, side, axis)
    return (kept.astype(F32) + recv.astype(F32)).astype(BF)


def reduce_chips(full, x_first):
    total, cols = full.shape
    n_seg = lax.axis_size("seg")
    seg = lax.axis_index("seg")
    side_y = lax.axis_index("rep") // 2
    cur = full.reshape(n_seg // 2, 2, 2, total // (2 * n_seg), cols)
    if x_first:
        cur = halve(cur, "seg", 1, seg % 2, 1)
        cur = halve(cur, "rep", 2, side_y, 1)
    else:
        cur = halve(cur, "rep", 2, side_y, 2)
        cur = halve(cur, "seg", 1, seg % 2, 1)
    for bit in reversed(seg_bits()):
        cur = cur.reshape((2, cur.shape[0] // 2) + cur.shape[1:])
        cur = halve(cur, "seg", bit, (seg // bit) % 2, 0)
    return cur.reshape(cur.shape[-2:])


def matmul(left, right):
    return jnp.dot(left, right, preferred_element_type=F32)


def matmul_rows(left, right):
    return lax.dot_general(left, right, (((0,), (0,)), ((), ())), preferred_element_type=F32)


def matmul_cols(left, right):
    return lax.dot_general(left, right, (((1,), (1,)), ((), ())), preferred_element_type=F32)


def norm_forward(values, gain):
    inverse = lax.rsqrt(jnp.mean(values * values, axis=-1, keepdims=True) + EPSILON)
    return (values * inverse * gain, inverse)


def norm_backward(values, inverse, gain, grad_out):
    normed = values * inverse
    scaled = grad_out * gain
    grad_values = inverse * (scaled - normed * jnp.mean(scaled * normed, axis=-1, keepdims=True))
    return (grad_values, normed)


def rope_tables(seg_len):
    position = jnp.arange(seg_len).astype(F32)
    freqs = ROPE_BASE ** (-(2.0 * jnp.arange(HD // 2).astype(F32)) / HD)
    angle = position[:, None] * freqs[None, :]
    cosine, sine = jnp.cos(angle), jnp.sin(angle)
    return (jnp.concatenate([cosine, cosine], -1), jnp.concatenate([-sine, sine], -1))


def rope_heads(values, cosine, sine):
    half = HD // 2
    swapped = jnp.concatenate([values[..., half:], values[..., :half]], -1)
    return values * cosine[:, None, :] + swapped * sine[:, None, :]


def mask_kernel(n_cols, cols_ref, out_ref, scratch):
    queries = cols_ref.shape[1]
    picks = cols_ref[0]
    pad = scratch.shape[0]
    high = lax.shift_right_arithmetic(picks, 7)
    low = jnp.bitwise_and(picks, LANES - 1)
    iota_high = lax.broadcasted_iota(jnp.int32, (pad, picks.shape[1]), 0)
    iota_low = lax.broadcasted_iota(jnp.int32, (LANES, picks.shape[1]), 0)
    for i in range(queries):
        hot_high = jnp.where(iota_high == high[i : i + 1, :], 1.0, 0.0).astype(BF)
        hot_low = jnp.where(iota_low == low[i : i + 1, :], 1.0, 0.0).astype(BF)
        scratch[:, i, :] = matmul_cols(hot_high, hot_low)
    out_ref[0] = jnp.where(scratch[0:n_cols] > 0.5, POS_BIG, NEG_BIG).astype(BF)


def build_mask(columns, n_cols):
    rows, queries, picks = columns.shape
    block = 16
    return pl.pallas_call(
        lambda *refs: mask_kernel(n_cols, *refs),
        grid=(rows, queries // block),
        in_specs=[pl.BlockSpec((1, block, picks), lambda r, g: (r, g, 0))],
        out_specs=pl.BlockSpec((1, n_cols, block, LANES), lambda r, g: (r, 0, g, 0)),
        out_shape=jax.ShapeDtypeStruct((rows, n_cols, queries, LANES), BF),
        scratch_shapes=[pltpu.VMEM((cdiv(n_cols, 8) * 8, block, LANES), F32)],
        compiler_params=pltpu.CompilerParams(vmem_limit_bytes=16 * 1024 * 1024),
        name="mask_build",
    )(columns)


def lane_blocks(value):
    return [value[:, i : i + LANES] for i in range(0, value.shape[1], LANES)]


def forward_kernel(n_pieces, q_ref, k_ref, v_ref, live_ref, mask_ref, *refs):
    pieces = refs[:n_pieces]
    o_ref, of_ref, p_ref, pl_ref, inv_ref, s_ref = refs[n_pieces:]
    scale = HD ** (-0.5)
    queries = q_ref[0]
    seg_len = queries.shape[0]
    row = lax.broadcasted_iota(jnp.int32, (seg_len, seg_len), 0)
    col = lax.broadcasted_iota(jnp.int32, (seg_len, seg_len), 1)
    allow = (col == row) | ((col < row) & (live_ref[0] == 1))
    s_local = jnp.where(allow, matmul_cols(queries, k_ref[0]) * scale, NEG_BIG)
    top = None
    per = pieces[0].shape[1] // LANES
    for t in range(n_pieces):
        scores = matmul_cols(queries, pieces[t][0]) * scale
        parts = lane_blocks(scores)
        for i in range(per):
            part = jnp.minimum(parts[i], mask_ref[0, t * per + i].astype(F32))
            s_ref[t, :, i * LANES : (i + 1) * LANES] = part
            top = part if top is None else jnp.maximum(top, part)
    row_max = jnp.max(s_local, axis=-1, keepdims=True)
    if top is not None:
        row_max = jnp.maximum(row_max, jnp.max(top, axis=-1, keepdims=True))
    e_local = jnp.exp(s_local - row_max)
    low = e_local.astype(BF)
    pl_ref[0, 0] = low
    acc = matmul(low, v_ref[0])
    total = None
    for t in range(n_pieces):
        expo = jnp.exp(s_ref[t] - row_max)
        for part in lane_blocks(expo):
            total = part if total is None else total + part
        low = expo.astype(BF)
        p_ref[0, 0, t] = low
        acc = acc + matmul(low, pieces[t][1])
    row_total = jnp.sum(e_local, axis=-1, keepdims=True)
    if total is not None:
        row_total = row_total + jnp.sum(total, axis=-1, keepdims=True)
    inverse = 1.0 / row_total
    out = acc * inverse
    of_ref[0] = out
    o_ref[0] = out.astype(BF)
    inv_ref[0, 0] = inverse


def backward_kernel(n_pieces, do_ref, of_ref, q_ref, k_ref, v_ref, inv_ref, pl_ref, p_ref, cos_ref, sin_ref, *refs):
    pieces = refs[:n_pieces]
    (d_ref,) = refs[n_pieces:]
    scale = HD ** (-0.5)
    d_out = do_ref[0]
    inverse = inv_ref[0, 0]
    delta = jnp.sum(d_out.astype(F32) * of_ref[0], axis=-1, keepdims=True)
    chances = pl_ref[0, 0].astype(F32) * inverse
    ds = (chances * (matmul_cols(d_out, v_ref[0]) - delta)).astype(BF)
    dq = matmul(ds, k_ref[0])
    dk = matmul_rows(ds, q_ref[0])
    dv = matmul_rows(chances.astype(BF), d_out)
    for t in range(n_pieces):
        dp = matmul_cols(d_out, pieces[t][1])
        ds = (p_ref[0, 0, t].astype(F32) * ((dp - delta) * inverse)).astype(BF)
        dq = dq + matmul(ds, pieces[t][0])
    cosine = cos_ref[...]
    sine = sin_ref[...]

    def back(value):
        return (value * cosine - pltpu.roll(value, HD // 2, 1) * sine) * scale

    d_ref[0, 0] = back(dq).astype(BF)
    d_ref[1, 0] = back(dk).astype(BF)
    d_ref[2, 0] = dv.astype(BF)


def attention_specs(n_pieces, piece_rows, seg_len):
    head = pl.BlockSpec((1, seg_len, HD), lambda h, r: (r, 0, h))
    piece = pl.BlockSpec((2, piece_rows, HD), lambda h, r: (0, 0, h))
    p_spec = pl.BlockSpec((1, 1, n_pieces, seg_len, piece_rows), lambda h, r: (r, h, 0, 0, 0))
    pl_spec = pl.BlockSpec((1, 1, seg_len, seg_len), lambda h, r: (r, h, 0, 0))
    inv_spec = pl.BlockSpec((1, 1, seg_len, 1), lambda h, r: (r, h, 0, 0))
    return head, piece, p_spec, pl_spec, inv_spec


def attention_forward(queries, keys, values, live, mask, pieces):
    rows, seg_len, width = queries.shape
    heads = width // HD
    n_pieces = len(pieces)
    piece_rows = pieces[0].shape[1]
    head, piece, p_spec, pl_spec, inv_spec = attention_specs(n_pieces, piece_rows, seg_len)
    flops = 4 * rows * heads * seg_len * HD * (n_pieces * piece_rows + seg_len)
    return pl.pallas_call(
        lambda *refs: forward_kernel(n_pieces, *refs),
        grid=(heads, rows),
        in_specs=[
            head,
            head,
            head,
            pl.BlockSpec((1, 1, seg_len), lambda h, r: (r, 0, 0)),
            pl.BlockSpec((1,) + mask.shape[1:], lambda h, r: (r, 0, 0, 0)),
        ]
        + [piece] * n_pieces,
        out_specs=[head, head, p_spec, pl_spec, inv_spec],
        out_shape=[
            jax.ShapeDtypeStruct(queries.shape, BF),
            jax.ShapeDtypeStruct(queries.shape, F32),
            jax.ShapeDtypeStruct((rows, heads, n_pieces, seg_len, piece_rows), BF),
            jax.ShapeDtypeStruct((rows, heads, seg_len, seg_len), BF),
            jax.ShapeDtypeStruct((rows, heads, seg_len, 1), F32),
        ],
        scratch_shapes=[pltpu.VMEM((n_pieces, seg_len, piece_rows), F32)],
        compiler_params=pltpu.CompilerParams(vmem_limit_bytes=40 * 1024 * 1024),
        cost_estimate=pl.CostEstimate(flops=8 * flops, bytes_accessed=20000000, transcendentals=flops // 512),
        name="attention_forward",
    )(queries, keys, values, live, mask, *pieces)


def attention_backward(d_out, out_f32, queries, keys, values, inverse, p_local, p_memory, cosine, sine, pieces):
    rows, seg_len, width = queries.shape
    heads = width // HD
    n_pieces = len(pieces)
    piece_rows = pieces[0].shape[1]
    head, piece, p_spec, pl_spec, inv_spec = attention_specs(n_pieces, piece_rows, seg_len)
    table = pl.BlockSpec((seg_len, HD), lambda h, r: (0, 0))
    flops = 4 * rows * heads * seg_len * HD * (n_pieces * piece_rows + seg_len)
    return pl.pallas_call(
        lambda *refs: backward_kernel(n_pieces, *refs),
        grid=(heads, rows),
        in_specs=[head, head, head, head, head, inv_spec, pl_spec, p_spec, table, table] + [piece] * n_pieces,
        out_specs=pl.BlockSpec((3, 1, seg_len, HD), lambda h, r: (0, r, 0, h)),
        out_shape=jax.ShapeDtypeStruct((3, rows, seg_len, width), BF),
        compiler_params=pltpu.CompilerParams(vmem_limit_bytes=40 * 1024 * 1024),
        cost_estimate=pl.CostEstimate(flops=8 * flops, bytes_accessed=20000000, transcendentals=0),
        name="attention_backward",
    )(d_out, out_f32, queries, keys, values, inverse, p_local, p_memory, cosine, sine, *pieces)


def allow_local_of(live):
    seg_len = live.shape[-1]
    position = jnp.arange(seg_len, dtype=jnp.int32)
    same = position[None, :] == position[:, None]
    return same[None] | ((position[None, :] < position[:, None])[None] & (live == 1))


def split_heads(value):
    rows, seg_len, width = value.shape
    return value.reshape(rows, seg_len, width // HD, HD)


def stream_forward(queries, keys, values, live, allow, memory):
    scale = HD ** (-0.5)
    q4, k4, v4 = split_heads(queries), split_heads(keys), split_heads(values)
    scores = jnp.einsum("rqhd,rkhd->rhqk", q4, k4, preferred_element_type=F32) * scale
    scores = jnp.where(allow_local_of(live)[:, None], scores, NEG_BIG)
    row_max = jnp.max(scores, axis=-1)
    expo = jnp.exp(scores - row_max[..., None])
    state = (
        row_max,
        jnp.sum(expo, axis=-1),
        jnp.einsum("rhqk,rkhd->rhqd", expo.astype(BF), v4, preferred_element_type=F32),
    )

    def step(running, item):
        row_max, row_total, acc = running
        block, allowed = item
        k3 = block[0].reshape(block.shape[1], -1, HD)
        v3 = block[1].reshape(block.shape[1], -1, HD)
        scores = jnp.einsum("rqhd,khd->rhqk", q4, k3, preferred_element_type=F32) * scale
        scores = jnp.where(allowed[:, None] > 0, scores, NEG_BIG)
        new_max = jnp.maximum(row_max, jnp.max(scores, axis=-1))
        shrink = jnp.exp(row_max - new_max)
        expo = jnp.exp(scores - new_max[..., None])
        acc = acc * shrink[..., None] + jnp.einsum(
            "rhqk,khd->rhqd", expo.astype(BF), v3, preferred_element_type=F32
        )
        return (new_max, row_total * shrink + jnp.sum(expo, axis=-1), acc), None

    (row_max, row_total, acc), unused = lax.scan(step, state, (memory, allow))
    out = (acc / row_total[..., None]).transpose(0, 2, 1, 3).reshape(queries.shape)
    return out.astype(BF), out, row_max + jnp.log(row_total)


def stream_backward(d_out, out_f32, queries, keys, values, live, log_total, allow, memory, cosine, sine):
    scale = HD ** (-0.5)
    q4, k4, v4, d4 = split_heads(queries), split_heads(keys), split_heads(values), split_heads(d_out)
    delta = jnp.sum(d4.astype(F32) * split_heads(out_f32), axis=-1).transpose(0, 2, 1)
    scores = jnp.einsum("rqhd,rkhd->rhqk", q4, k4, preferred_element_type=F32) * scale
    scores = jnp.where(allow_local_of(live)[:, None], scores, NEG_BIG)
    chances = jnp.exp(scores - log_total[..., None])
    dp = jnp.einsum("rqhd,rkhd->rhqk", d4, v4, preferred_element_type=F32)
    ds = (chances * (dp - delta[..., None])).astype(BF)
    dq = jnp.einsum("rhqk,rkhd->rqhd", ds, k4, preferred_element_type=F32)
    dk = jnp.einsum("rhqk,rqhd->rkhd", ds, q4, preferred_element_type=F32)
    dv = jnp.einsum("rhqk,rqhd->rkhd", chances.astype(BF), d4, preferred_element_type=F32)

    def step(running, item):
        block, allowed = item
        k3 = block[0].reshape(block.shape[1], -1, HD)
        v3 = block[1].reshape(block.shape[1], -1, HD)
        scores = jnp.einsum("rqhd,khd->rhqk", q4, k3, preferred_element_type=F32) * scale
        scores = jnp.where(allowed[:, None] > 0, scores, NEG_BIG)
        chances = jnp.exp(scores - log_total[..., None])
        dp = jnp.einsum("rqhd,khd->rhqk", d4, v3, preferred_element_type=F32)
        ds = (chances * (dp - delta[..., None])).astype(BF)
        return running + jnp.einsum("rhqk,khd->rqhd", ds, k3, preferred_element_type=F32), None

    dq, unused = lax.scan(step, dq, (memory, allow))

    def back(value):
        turned = rope_heads(value.reshape((-1,) + value.shape[2:]), jnp.tile(cosine, (value.shape[0], 1)), -jnp.tile(sine, (value.shape[0], 1)))
        return (turned * scale).reshape(queries.shape).astype(BF)

    return jnp.stack([back(dq), back(dk), dv.reshape(queries.shape).astype(BF)])


def local(
    layer_input,
    live,
    knn_index,
    mem_keys,
    mem_values,
    gain_attn,
    w_query,
    w_key,
    w_value,
    w_out,
    gain_ffn,
    w_gate,
    w_up,
    w_down,
    cotangent,
):
    seg_len, width = layer_input.shape[1:]
    half = width // 2
    ff = w_gate.shape[1]
    ff_half = ff // 2
    n_seg = lax.axis_size("seg")
    tokens = seg_len * n_seg
    seg = lax.axis_index("seg")
    core = lax.axis_index("rep") % 2
    n_z = n_seg // 2
    use_kernel = n_seg <= KERNEL_SEGMENTS

    def cut(value, index, size):
        return lax.dynamic_slice_in_dim(value, index * size, size, value.ndim - 1)

    def trade_columns(value):
        size = value.shape[-1] // 2
        return ordered(cut(value, core, size), core_swap(cut(value, 1 - core, size)), core, 0)

    def both_rows(value):
        return jnp.concatenate([value[None], core_swap(value)[None]], 0)

    def gain_columns(a, b):
        return jnp.concatenate([a[:, None], b[:, None], jnp.zeros((a.shape[0], LANES - 2), BF)], 1)

    def thirds(value, index):
        return cut(value, index, half)

    gains = gain_columns(gain_attn, gain_ffn)
    mine = jnp.concatenate([thirds(w_query, core), thirds(w_key, core), thirds(w_value, core), gains], 1)
    theirs = jnp.concatenate(
        [thirds(w_query, 1 - core), thirds(w_key, 1 - core), thirds(w_value, 1 - core), gains], 1
    )
    w_qkv_all = gather_chips(ordered(mine, core_swap(theirs), core, 0))
    w_qkv = w_qkv_all[:, : 3 * half]
    g_attn = w_qkv_all[:, 3 * half].astype(F32)
    g_ffn = w_qkv_all[:, 3 * half + 1].astype(F32)

    memory = jnp.stack([mem_keys[0], mem_values[0]])
    kv = jnp.concatenate([cut(memory, core, half), core_swap(cut(memory, 1 - core, half))], 1)

    coded = both_rows(knn_index[0] * 2 + live[0][:, None])
    live_both = jnp.bitwise_and(coded[:, :, 0], 1)[:, None, :]
    picks = lax.shift_right_arithmetic(coded, 1)
    pair = picks >= tokens
    slot = jnp.where(pair, picks - tokens, picks)
    slot_seg = slot // seg_len
    swapped = jnp.arange(2, dtype=jnp.int32)[:, None, None]
    kv_row = jnp.bitwise_xor(pair.astype(jnp.int32), swapped)
    within = kv_row * seg_len + (slot - slot_seg * seg_len)
    kv_rows = 2 * seg_len

    if use_kernel:
        distance = seg // 2 - slot_seg // 2
        piece_no = jnp.where(slot_seg % 2 == seg % 2, distance - 1, n_z - 1 + distance)
        columns = jnp.where(picks >= 0, piece_no * kv_rows + within, -1)
        mask = build_mask(columns, (2 * n_z - 1) * kv_rows // LANES)
        hops = [kv]
        for unused in range(n_z - 1):
            hops.append(lax.ppermute(hops[-1], "seg", [(i, i + 2) for i in range(n_seg - 2)]))
        across = [lax.ppermute(kv, "seg", [(i, i + 1) for i in range(0, n_seg, 2)])]
        across += [flip(piece, "seg", 1) for piece in hops[1:]]
        pieces = hops[1:] + across
    else:
        columns = jnp.where(picks >= 0, slot_seg * kv_rows + within, n_seg * kv_rows)
        rows_at = jnp.arange(2)[:, None, None]
        queries_at = jnp.arange(seg_len)[None, :, None]
        allow = jnp.zeros((2, seg_len, n_seg * kv_rows), BF).at[rows_at, queries_at, columns].set(1.0, mode="drop")
        allow = allow.reshape(2, seg_len, n_seg, kv_rows).transpose(2, 0, 1, 3)
        gathered = lax.all_gather(kv, "seg", axis=0)

    gate_up = jnp.concatenate([trade_columns(w_gate), trade_columns(w_up)], 1)
    w_o_all = gather_chips(trade_columns(w_out))
    gate_up_all = gather_chips(gate_up)
    w_d_all = gather_chips(trade_columns(w_down))
    wg = gate_up_all[:, :ff_half]
    wu = gate_up_all[:, ff_half:]

    def own_rows(value):
        size = value.shape[0] // 2
        pairs = value.reshape(2, size, value.shape[1])
        return ordered(pick(pairs, core, 0), core_swap(pick(pairs, 1 - core, 0)), core, 1)

    wo = own_rows(w_o_all)
    wd = own_rows(w_d_all)

    x_both = both_rows(layer_input[0])
    g_both = both_rows(cotangent[0])
    x_float = x_both.reshape(2 * seg_len, width).astype(F32)
    grad_out = g_both.reshape(2 * seg_len, width)
    cosine, sine = rope_tables(seg_len)
    cos_two = jnp.tile(cosine, (2, 1))
    sin_two = jnp.tile(sine, (2, 1))
    h_float, inv_one = norm_forward(x_float, g_attn)
    h_one = h_float.astype(BF)
    qkv = matmul(h_one, w_qkv)
    heads_here = half // HD
    turned = rope_heads(qkv[:, : 2 * half].reshape(2 * seg_len, 2 * heads_here, HD), cos_two, sin_two)
    turned = turned.reshape(2 * seg_len, 2 * half).astype(BF)
    queries = turned[:, :half].reshape(2, seg_len, half)
    keys = turned[:, half:].reshape(2, seg_len, half)
    values = qkv[:, 2 * half :].astype(BF).reshape(2, seg_len, half)
    if use_kernel:
        out_low, out_f32, p_memory, p_local, inverse = attention_forward(
            queries, keys, values, live_both, mask, pieces
        )
    else:
        out_low, out_f32, log_total = stream_forward(queries, keys, values, live_both, allow, gathered)
    attended = out_low.reshape(2 * seg_len, half)

    def both_sums(part):
        low = part.astype(BF)
        other = core_swap(jnp.concatenate([low[seg_len:], low[:seg_len]], 0))
        return low.astype(F32) + other.astype(F32)

    x_one = x_float + both_sums(matmul(attended, wo))
    h_two_f, inv_two = norm_forward(x_one, g_ffn)
    h_two = h_two_f.astype(BF)
    gate = matmul(h_two, wg)
    upward = matmul(h_two, wu)
    sigma = jax.nn.sigmoid(gate)
    swish = gate * sigma
    hidden = (swish * upward).astype(BF)
    down = matmul(hidden, wd)
    layer_output = (x_one[:seg_len] + down[:seg_len] + core_swap(down[seg_len:].astype(BF)).astype(F32)).astype(BF)

    hidden_all = ordered(hidden, core_swap_rows(hidden, seg_len), core, 1)
    grad_wd = matmul_rows(hidden_all, cut(grad_out, core, half)).astype(BF)
    d_hidden = matmul_cols(grad_out, wd)
    d_gate = (d_hidden * upward * sigma * (1.0 + gate * (1.0 - sigma))).astype(BF)
    d_up = (d_hidden * swish).astype(BF)
    grad_wg = matmul_rows(h_two, d_gate).astype(BF)
    grad_wu = matmul_rows(h_two, d_up).astype(BF)
    d_h_two = both_sums(matmul_cols(d_gate, wg) + matmul_cols(d_up, wu))
    d_x_norm, normed_two = norm_backward(x_one, inv_two, g_ffn, d_h_two)
    grad_g_ffn = jnp.sum(d_h_two[:seg_len] * normed_two[:seg_len], axis=0)
    d_x_one = grad_out.astype(F32) + d_x_norm
    d_branch = d_x_one.astype(BF)
    attended_all = ordered(attended, core_swap_rows(attended, seg_len), core, 1)
    grad_wo = matmul_rows(attended_all, cut(d_branch, core, half)).astype(BF)
    d_att = matmul_cols(d_branch, wo).astype(BF).reshape(2, seg_len, half)

    if use_kernel:
        d_qkv = attention_backward(
            d_att, out_f32, queries, keys, values, inverse, p_local, p_memory, cosine, sine, pieces
        )
    else:
        d_qkv = stream_backward(
            d_att, out_f32, queries, keys, values, live_both, log_total, allow, gathered, cosine, sine
        )
    d_qkv = d_qkv.reshape(3, 2 * seg_len, half).transpose(1, 0, 2).reshape(2 * seg_len, 3 * half)
    grad_qkv = matmul_rows(h_one, d_qkv).astype(BF)
    part = matmul_cols(d_qkv, w_qkv)
    d_h_one = part[:seg_len] + core_swap(part[seg_len:].astype(BF)).astype(F32)
    x_own = x_float[:seg_len]
    d_x_first, normed_one = norm_backward(x_own, inv_one[:seg_len], g_attn, d_h_one)
    grad_g_attn = jnp.sum(d_h_one * normed_one, axis=0)
    grad_x = (d_x_one[:seg_len] + d_x_first).astype(BF)

    def finish(value):
        size = value.shape[0] // 2
        pairs = value.reshape(2, size, value.shape[1])
        return pick(pairs, core, 0), core_swap(pick(pairs, 1 - core, 0))

    def whole(value):
        mine, other = finish(value)
        return ordered(mine, other, core, 1).astype(F32)

    sum_wd = whole(reduce_chips(grad_wd, True))
    sum_wg = whole(reduce_chips(grad_wg, True))
    sum_wu = whole(reduce_chips(grad_wu, False))
    sum_wo = whole(reduce_chips(grad_wo, False))
    grad_qkv = jnp.concatenate([grad_qkv, gain_columns(grad_g_attn.astype(BF), grad_g_ffn.astype(BF))], 1)
    mine, other = finish(reduce_chips(grad_qkv, False))

    def third(i):
        return ordered(mine[:, i * half : (i + 1) * half], other[:, i * half : (i + 1) * half], core, 1).astype(F32)

    sum_gains = mine[:, 3 * half : 3 * half + 2].astype(F32) + other[:, 3 * half : 3 * half + 2].astype(F32)
    return (
        layer_output[None],
        grad_x[None],
        sum_gains[:, 0],
        third(0),
        third(1),
        third(2),
        sum_wo,
        sum_gains[:, 1],
        sum_wg,
        sum_wu,
        sum_wd,
    )


def core_swap_rows(value, seg_len):
    return core_swap(jnp.concatenate([value[seg_len:], value[:seg_len]], 0))


def solution(mesh):
    tokens = P("rep", "seg", None)
    vector = P(("seg", "rep"))
    matrix = P(("seg", "rep"), None)
    return jax.shard_map(
        local,
        mesh=mesh,
        in_specs=(
            tokens,
            P("rep", "seg"),
            tokens,
            tokens,
            tokens,
            vector,
            matrix,
            matrix,
            matrix,
            matrix,
            vector,
            matrix,
            matrix,
            matrix,
            tokens,
        ),
        out_specs=(tokens, tokens, vector, matrix, matrix, matrix, matrix, vector, matrix, matrix, matrix),
        check_vma=False,
    )
```

time: 1450 us -> 526 us (0.36)
  waiting for transfers between devices: 901 us -> 277 us
  local copies, waits for them, and re-layouts: 228 us -> 31.9 us
  matrix products: 141 us -> 31.4 us
  blocking collectives: 47.7 us -> 0 us
  Pallas kernels: 0 us -> 41.7 us
  starting transfers between devices: 42.4 us -> 78 us
    all_to_all x9 -> x0, waiting for transfers between devices: 521 us -> none  [the longest x1 121 us: local(): lax.all_to_all(grad_wu.astype(jnp.bfloat16), 'seg', split_axis=0, concat_...]
    all_gather x11 -> x0, waiting for transfers between devices: 372 us -> none  [the longest x1 65.4 us: local(): lax.all_gather(shards[6], ('seg', 'rep'), axis=0, tiled=True)]
    ppermute x2 -> x65, waiting for transfers between devices: 3.12 us -> 277 us  [the longest x61 255 us: flip(): return lax.ppermute(value, axis, [(i, i ^ bit) for i in range(count)])]
    unnamed x89 -> x118, local copies, waits for them, and re-layouts: 175 us -> 5.69 us
    dot_general x55 -> x5, matrix products: 90.2 us -> 10.4 us  [matmul(): return jnp.dot(left, right, preferred_element_type=F32)]
    ppermute x2 -> x65, starting transfers between devices: 0.96 us -> 78 us  [the longest x61 57.3 us: flip(): return lax.ppermute(value, axis, [(i, i ^ bit) for i in range(count)])]
    unnamed x2 -> x0, blocking collectives: 47.7 us -> none
    pallas_call x0 -> x3, Pallas kernels: none -> 41.7 us  [the longest x1 17.2 us: attention_backward(): pl.pallas_call(lambda *refs: backward_kernel(n_pieces, *refs), grid=(head...]
  transfers between devices with their start and end apart: 29 -> 65, of which waited for: 18 -> 32; matrix products, arithmetic and copies ran while one was open for 24% -> 18% of each run, Pallas kernels for 0% -> 8%
where the time goes in v1:
time: 526 us; the launch traced here: 518 us
  waiting for transfers between devices  277 us (53%)
  starting transfers between devices  78 us (15%)
  other arithmetic  56.1 us (11%)
  Pallas kernels  41.7 us (8%)
  local copies, waits for them, and re-layouts  31.9 us (6%)
  matrix products  31.4 us (6%)
    ppermute x61, waiting for transfers between devices, flip(): return lax.ppermute(value, axis, [(i, i ^ bit) for i in range(count)])  255 us
    ppermute x61, starting transfers between devices, flip(): return lax.ppermute(value, axis, [(i, i ^ bit) for i in range(count)])  57.3 us
    ppermute x3, waiting for transfers between devices, local(): lax.ppermute(hops[-1], 'seg', [(i, i + 2) for i in range(n_seg - 2)])  21.9 us
    ppermute x3, starting transfers between devices, local(): lax.ppermute(hops[-1], 'seg', [(i, i + 2) for i in range(n_seg - 2)])  18.1 us
    pallas_call x1, Pallas kernels, attention_backward(): pl.pallas_call(lambda *refs: backward_kernel(n_pieces, *refs), grid=(head...  17.2 us
    pallas_call x1, Pallas kernels, attention_forward(): pl.pallas_call(lambda *refs: forward_kernel(n_pieces, *refs), grid=(heads...  13.8 us
    select_n x30, other arithmetic, ordered(): first = jnp.where(bit == 0, mine, other)  12.6 us
    dot_general x5, matrix products, matmul_rows(): lax.dot_general(left, right, (((0,), (0,)), ((), ())), preferred_element_...  10.9 us
  transfers between devices with their start and end apart: 65, of which 32 were waited for; matrix products, arithmetic and copies ran while one was open for 18% of the time, Pallas kernels for 8%

profile of v1, /device:TPU:0, one launch (start us, length us, event | category | flops | bytes accessed | tf_op | source)
XLA Modules:
  0.0 518.3 jit_solution(5865691273722765975)
XLA Ops:
  24.9 10.6 %mask_build.1.refs_4_ = bf16[2,21,192,128]{3,2,1,0:T(8,128)(2,1)S(1)} custom-call(s32[2,192,128]{2,1,0:T(8,128)S(1)} %copy.37.refs_0_), custom_call_target="tpu_custom_call" | custom-call | tf_op jit(solution)/shard_map/mask_build/pallas_call | solution.py:146
  39.2 5.6 %collective-permute-done.17 = bf16[2,1,64,512]{3,2,0,1:T(8,128)(2,1)S(1)} collective-permute-done((bf16[2,1,64,512]{3,2,0,1:T(8,128)(2,1)S(1)}, bf16[2,1,64,512]{3,2,0,1:T(8,128)(2,1)S(1)}, u32[]{:S(2)}, u32[]{:S(2)}) %collective-permute-start.17) | collective-permute-done | bytes 131104 | tf_op jit(solution)/shard_map/ppermute | solution.py:27
  50.1 9.8 %collective-permute-done.2 = bf16[1,1,64,1664]{3,2,0,1:T(8,128)(2,1)S(1)} collective-permute-done((bf16[1,1,64,1664]{3,2,0,1:T(8,128)(2,1)S(1)}, bf16[1,1,64,1664]{3,2,0,1:T(8,128)(2,1)S(1)}, u32[]{:S(2)}, u32[]{:S(2)}) %collective-permute-start.2) | collective-permute-done | bytes 213024 | tf_op jit(solution)/shard_map/ppermute | solution.py:27
  79.6 25.6 %collective-permute-done.30 = bf16[2,1,176,512]{3,2,0,1:T(8,128)(2,1)} collective-permute-done((bf16[2,1,176,512]{3,2,0,1:T(8,128)(2,1)}, bf16[2,1,176,512]{3,2,0,1:T(8,128)(2,1)}, u32[]{:S(2)}, u32[]{:S(2)}) %collective-permute-start.30) | collective-permute-done | bytes 360480 | tf_op jit(solution)/shard_map/ppermute | solution.py:27
  107.9 6.3 %collective-permute-done.3 = bf16[2,1,64,1664]{3,2,0,1:T(8,128)(2,1)S(1)} collective-permute-done((bf16[2,1,64,1664]{3,2,0,1:T(8,128)(2,1)}, bf16[2,1,64,1664]{3,2,0,1:T(8,128)(2,1)S(1)}, u32[]{:S(2)}, u32[]{:S(2)}) %collective-permute-start.3) | collective-permute-done | bytes 426016 | tf_op jit(solution)/shard_map/ppermute | solution.py:27
  119.6 9.9 %collective-permute-done.25 = bf16[2,1,64,2816]{3,2,0,1:T(8,128)(2,1)S(1)} collective-permute-done((bf16[2,1,64,2816]{3,2,0,1:T(8,128)(2,1)S(1)}, bf16[2,1,64,2816]{3,2,0,1:T(8,128)(2,1)S(1)}, u32[]{:S(2)}, u32[]{:S(2)}) %collective-permute-start.25) | collective-permute-done | bytes 720928 | tf_op jit(solution)/shard_map/ppermute | solution.py:27
  133.3 14.4 %collective-permute-start.9 = (bf16[2,384,512]{2,1,0:T(8,128)(2,1)S(1)}, bf16[2,384,512]{2,1,0:T(8,128)(2,1)S(1)}, u32[]{:S(2)}, u32[]{:S(2)}) collective-permute-start(bf16[2,384,512]{2,1,0:T(8,128)(2,1)S(1)} %collective-permute-done.8.refs_5_.refs_10_), channel_id=1, source_target_pairs={{0,8},{4,12},{8,16},{12,20},{16,24},{20,28},{1,9},{5,13},{9,17},{1... | collective-permute-start | bytes 2359304 | tf_op jit(solution)/shard_map/ppermute | solution.py:448
  153.4 11.4 %collective-permute-done.9.refs_6_.refs_11_ = bf16[2,384,512]{2,1,0:T(8,128)(2,1)S(1)} collective-permute-done((bf16[2,384,512]{2,1,0:T(8,128)(2,1)S(1)}, bf16[2,384,512]{2,1,0:T(8,128)(2,1)S(1)}, u32[]{:S(2)}, u32[]{:S(2)}) %collective-permute-start.9) | collective-permute-done | bytes 786464 | tf_op jit(solution)/shard_map/ppermute | solution.py:448
  166.4 16.1 %collective-permute-done.26 = bf16[4,1,1,64,2816]{4,3,2,1,0:T(8,128)(2,1)S(1)} collective-permute-done((bf16[4,1,1,64,2816]{4,3,2,1,0:T(8,128)(2,1)S(1)}, bf16[4,1,1,64,2816]{4,3,2,1,0:T(8,128)(2,1)S(1)}, u32[]{:S(2)}, u32[]{:S(2)}) %collective-permute-start.26) | collective-permute-done | bytes 1441824 | tf_op jit(solution)/shard_map/ppermute | solution.py:27
  188.3 10.5 %collective-permute-done.10.refs_7_.refs_12_ = bf16[2,384,512]{2,1,0:T(8,128)(2,1)S(1)} collective-permute-done((bf16[2,384,512]{2,1,0:T(8,128)(2,1)S(1)}, bf16[2,384,512]{2,1,0:T(8,128)(2,1)S(1)}, u32[]{:S(2)}, u32[]{:S(2)}) %collective-permute-start.10) | collective-permute-done | bytes 786464 | tf_op jit(solution)/shard_map/ppermute | solution.py:448
  200.3 22.3 %collective-permute-done.5 = bf16[4,2,1,64,1664]{4,3,2,1,0:T(8,128)(2,1)S(1)} collective-permute-done((bf16[4,2,1,64,1664]{4,3,2,1,0:T(8,128)(2,1)S(1)}, bf16[4,2,1,64,1664]{4,3,2,1,0:T(8,128)(2,1)S(1)}, u32[]{:S(2)}, u32[]{:S(2)}) %collective-permute-start.5) | collective-permute-done | bytes 1703968 | tf_op jit(solution)/shard_map/ppermute | solution.py:27
  229.7 7.4 %collective-permute-done.14.refs_11_.refs_16_ = bf16[2,384,512]{2,1,0:T(8,128)(2,1)S(1)} collective-permute-done((bf16[2,384,512]{2,1,0:T(8,128)(2,1)S(1)}, bf16[2,384,512]{2,1,0:T(8,128)(2,1)S(1)}, u32[]{:S(2)}, u32[]{:S(2)}) %collective-permute-start.14) | collective-permute-done | bytes 786464 | tf_op jit(solution)/shard_map/ppermute | solution.py:27
  237.2 13.8 %attention_forward.1 = (bf16[2,192,512]{2,1,0:T(8,128)(2,1)S(1)}, f32[2,192,512]{2,1,0:T(8,128)S(1)}, bf16[2,4,7,192,384]{4,3,2,1,0:T(8,128)(2,1)}, bf16[2,4,192...) custom-call(bf16[2,192,512]{2,1,0:T(8,128)(2,1)S(1)} %bitcast.269, bf16[2,192,512]{2,1,0:T(8,128)(2,1)S(1)} %bitcast.267, ...), custom_call_target="tpu_custom_call" | custom-call | flops 18119393280 | bytes 20000000 | tf_op jit(solution)/shard_map/attention_forward/pallas_call | solution.py:249
  258.5 23.5 %collective-permute-done.27 = bf16[4,2,1,64,2816]{4,3,2,1,0:T(8,128)(2,1)} collective-permute-done((bf16[4,2,1,64,2816]{4,3,2,1,0:T(8,128)(2,1)}, bf16[4,2,1,64,2816]{4,3,2,1,0:T(8,128)(2,1)}, u32[]{:S(2)}, u32[]{:S(2)}) %collective-permute-start.27) | collective-permute-done | bytes 2883616 | tf_op jit(solution)/shard_map/ppermute | solution.py:27
  314.0 17.2 %attention_backward.1 = bf16[3,2,192,512]{3,2,1,0:T(8,128)(2,1)S(1)} custom-call(bf16[2,192,512]{2,1,0:T(8,128)(2,1)S(1)} %bitcast.271, f32[2,192,512]{2,1,0:T(8,128)S(1)} %get-tuple-element.17.refs_1_, bf16[2,192,512]{2,1,0:T(8,128)(2,1)S(1)} %bitcast.270, bf16[2,192,512]{2,1,0:T(8,128)(2,1)S(1)} %bitcast.268, bf16[2,192,512]{2,1,0:T(8,128)(2,1)S(1)} %bitcast.266, ...), custom_call_target="tpu_custom_call" | custom-call | flops 18119393280 | bytes 20000000 | tf_op jit(solution)/shard_map/attention_backward/pallas_call | solution.py:283
  369.0 21.7 %collective-permute-done.45 = bf16[4,64,512]{2,1,0:T(8,128)(2,1)S(1)} collective-permute-done((bf16[4,64,512]{2,1,0:T(8,128)(2,1)S(1)}, bf16[4,64,512]{2,1,0:T(8,128)(2,1)S(1)}, u32[]{:S(2)}, u32[]{:S(2)}) %collective-permute-start.45) | collective-permute-done | bytes 262176 | tf_op jit(solution)/shard_map/ppermute | solution.py:27
  405.5 9.2 %collective-permute-done.50 = bf16[4,64,1408]{2,1,0:T(8,128)(2,1)S(1)} collective-permute-done((bf16[4,64,1408]{2,1,0:T(8,128)(2,1)S(1)}, bf16[4,64,1408]{2,1,0:T(8,128)(2,1)S(1)}, u32[]{:S(2)}, u32[]{:S(2)}) %collective-permute-start.50) | collective-permute-done | bytes 720928 | tf_op jit(solution)/shard_map/ppermute | solution.py:27
  423.7 16.4 %collective-permute-done.51 = bf16[2,64,1408]{2,1,0:T(8,128)(2,1)S(1)} collective-permute-done((bf16[2,64,1408]{2,1,0:T(8,128)(2,1)S(1)}, bf16[2,64,1408]{2,1,0:T(8,128)(2,1)S(1)}, u32[]{:S(2)}, u32[]{:S(2)}) %collective-permute-start.51) | collective-permute-done | bytes 360480 | tf_op jit(solution)/shard_map/ppermute | solution.py:27
  442.0 5.8 %collective-permute-done.56 = bf16[2,64,1408]{2,1,0:T(8,128)(2,1)S(1)} collective-permute-done((bf16[2,64,1408]{2,1,0:T(8,128)(2,1)S(1)}, bf16[2,64,1408]{2,1,0:T(8,128)(2,1)S(1)}, u32[]{:S(2)}, u32[]{:S(2)}) %collective-permute-start.56) | collective-permute-done | bytes 360480 | tf_op jit(solution)/shard_map/ppermute | solution.py:27
  458.1 10.0 %collective-permute-done.61 = bf16[4,176,512]{2,1,0:T(8,128)(2,1)S(1)} collective-permute-done((bf16[4,176,512]{2,1,0:T(8,128)(2,1)S(1)}, bf16[4,176,512]{2,1,0:T(8,128)(2,1)S(1)}, u32[]{:S(2)}, u32[]{:S(2)}) %collective-permute-start.61) | collective-permute-done | bytes 720928 | tf_op jit(solution)/shard_map/ppermute | solution.py:27
  470.1 16.2 %collective-permute-done.62 = bf16[2,176,512]{2,1,0:T(8,128)(2,1)S(1)} collective-permute-done((bf16[2,176,512]{2,1,0:T(8,128)(2,1)S(1)}, bf16[2,176,512]{2,1,0:T(8,128)(2,1)S(1)}, u32[]{:S(2)}, u32[]{:S(2)}) %collective-permute-start.62) | collective-permute-done | bytes 360480 | tf_op jit(solution)/shard_map/ppermute | solution.py:27
  489.4 5.6 %collective-permute-done.63 = bf16[1,176,512]{2,1,0:T(8,128)(2,1)S(1)} collective-permute-done((bf16[1,176,512]{2,1,0:T(8,128)(2,1)S(1)}, bf16[1,176,512]{2,1,0:T(8,128)(2,1)S(1)}, u32[]{:S(2)}, u32[]{:S(2)}) %collective-permute-start.63) | collective-permute-done | bytes 180256 | tf_op jit(solution)/shard_map/ppermute | solution.py:27
  495.2 12.7 %collective-permute-done.40 = bf16[2,64,1664]{2,1,0:T(8,128)(2,1)S(1)} collective-permute-done((bf16[2,64,1664]{2,1,0:T(8,128)(2,1)S(1)}, bf16[2,64,1664]{2,1,0:T(8,128)(2,1)S(1)}, u32[]{:S(2)}, u32[]{:S(2)}) %collective-permute-start.40) | collective-permute-done | bytes 426016 | tf_op jit(solution)/shard_map/ppermute | solution.py:27
  508.2 5.8 %collective-permute-done.41 = bf16[1,64,1664]{2,1,0:T(8,128)(2,1)S(1)} collective-permute-done((bf16[1,64,1664]{2,1,0:T(8,128)(2,1)S(1)}, bf16[1,64,1664]{2,1,0:T(8,128)(2,1)S(1)}, u32[]{:S(2)}, u32[]{:S(2)}) %collective-permute-start.41) | collective-permute-done | bytes 213024 | tf_op jit(solution)/shard_map/ppermute | solution.py:27
  (414 shorter events, 207.7 us)
Async XLA Ops:
  0.7 66.2 %collective-permute-start.35 = (bf16[192,1024]{1,0:T(8,128)(2,1)}, bf16[192,1024]{1,0:T(8,128)(2,1)}, u32[]{:S(2)}, u32[]{:S(2)}) collective-permute-start(bf16[192,1024]{1,0:T(8,128)(2,1)} %bitcast.327), channel_id=1, source_target_pairs={{0,1},{1,0},{2,3},{3,2},{4,5},{5,4},{6,7},{7,6},{8,9},{9,8},{10,11... | collective-permute-start | bytes 1179656 | tf_op jit(solution)/shard_map/ppermute | solution.py:27
  6.1 29.5 %collective-permute-start.1 = (bf16[32,1664]{1,0:T(8,128)(2,1)}, bf16[32,1664]{1,0:T(8,128)(2,1)}, u32[]{:S(2)}, u32[]{:S(2)}) collective-permute-start(bf16[32,1664]{1,0:T(8,128)(2,1)} %concatenate.149), channel_id=1, source_target_pairs={{0,1},{1,0},{2,3},{3,2},{4,5},{5,4},{6,7},{7,6},{8,9},{9,8},{10,11... | collective-permute-start | bytes 319496 | tf_op jit(solution)/shard_map/ppermute | solution.py:27
  6.4 55.9 %collective-permute-start = (bf16[192,1024]{1,0:T(8,128)(2,1)}, bf16[192,1024]{1,0:T(8,128)(2,1)S(1)}, u32[]{:S(2)}, u32[]{:S(2)}) collective-permute-start(bf16[192,1024]{1,0:T(8,128)(2,1)} %bitcast.275), channel_id=1, source_target_pairs={{0,1},{1,0},{2,3},{3,2},{4,5},{5,4},{6,7},{7,6},{8,9},{9,8},{10,11... | collective-permute-start | bytes 1179656 | tf_op jit(solution)/shard_map/ppermute | solution.py:27
  21.6 41.9 %collective-permute-start.7 = (bf16[2,192,512]{2,1,0:T(8,128)(2,1)}, bf16[2,192,512]{2,1,0:T(8,128)(2,1)}, u32[]{:S(2)}, u32[]{:S(2)}) collective-permute-start(bf16[2,192,512]{2,1,0:T(8,128)(2,1)} %get-tuple-element.73), channel_id=1, source_target_pairs={{0,1},{1,0},{2,3},{3,2},{4,5},{5,4},{6,7},{7,6},{8,9},{9,8},{10,11... | collective-permute-start | bytes 1179656 | tf_op jit(solution)/shard_map/ppermute | solution.py:27
  44.8 27.6 %collective-permute-start.24 = (bf16[1,1,64,2816]{3,2,0,1:T(8,128)(2,1)}, bf16[1,1,64,2816]{3,2,0,1:T(8,128)(2,1)}, u32[]{:S(2)}, u32[]{:S(2)}) collective-permute-start(bf16[1,1,64,2816]{3,2,0,1:T(8,128)(2,1)} %maximum_bitcast_fusion.3), channel_id=1, source_target_pairs={{0,8},{4,12},{8,0},{12,4},{16,24},{20,28},{24,16},{28,20},{1,9},{5... | collective-permute-start | bytes 1081352 | tf_op jit(solution)/shard_map/ppermute | solution.py:27
  62.4 42.9 %collective-permute-start.30 = (bf16[2,1,176,512]{3,2,0,1:T(8,128)(2,1)}, bf16[2,1,176,512]{3,2,0,1:T(8,128)(2,1)}, u32[]{:S(2)}, u32[]{:S(2)}) collective-permute-start(bf16[2,1,176,512]{3,2,0,1:T(8,128)(2,1)} %pad_maximum_fusion.23), channel_id=1, source_target_pairs={{0,16},{4,20},{8,24},{12,28},{16,0},{20,4},{24,8},{28,12},{1,17},{... | collective-permute-start | bytes 1081352 | tf_op jit(solution)/shard_map/ppermute | solution.py:27
  63.5 50.8 %collective-permute-start.3 = (bf16[2,1,64,1664]{3,2,0,1:T(8,128)(2,1)}, bf16[2,1,64,1664]{3,2,0,1:T(8,128)(2,1)S(1)}, u32[]{:S(2)}, u32[]{:S(2)}) collective-permute-start(bf16[2,1,64,1664]{3,2,0,1:T(8,128)(2,1)} %pad_maximum_fusion.21), channel_id=1, source_target_pairs={{0,16},{4,20},{8,24},{12,28},{16,0},{20,4},{24,8},{28,12},{1,17},{... | collective-permute-start | bytes 1277960 | tf_op jit(solution)/shard_map/ppermute | solution.py:27
  66.9 63.0 %collective-permute-start.8 = (bf16[2,384,512]{2,1,0:T(8,128)(2,1)S(1)}, bf16[2,384,512]{2,1,0:T(8,128)(2,1)S(1)}, u32[]{:S(2)}, u32[]{:S(2)}) collective-permute-start(bf16[2,384,512]{2,1,0:T(8,128)(2,1)S(1)} %pad_maximum_fusion.13), channel_id=1, source_target_pairs={{0,8},{4,12},{8,16},{12,20},{16,24},{20,28},{1,9},{5,13},{9,17},{1... | collective-permute-start | bytes 2359304 | tf_op jit(solution)/shard_map/ppermute | solution.py:448
  72.4 157.2 %collective-permute-start.11 = (bf16[2,384,512]{2,1,0:T(8,128)(2,1)S(1)}, bf16[2,384,512]{2,1,0:T(8,128)(2,1)S(1)}, u32[]{:S(2)}, u32[]{:S(2)}) collective-permute-start(bf16[2,384,512]{2,1,0:T(8,128)(2,1)S(1)} %pad_maximum_fusion.13), channel_id=1, source_target_pairs={{0,4},{8,12},{16,20},{24,28},{1,5},{9,13},{17,21},{25,29},{2,6},{1... | collective-permute-start | bytes 2359304 | tf_op jit(solution)/shard_map/ppermute | solution.py:449
  76.3 53.3 %collective-permute-start.25 = (bf16[2,1,64,2816]{3,2,0,1:T(8,128)(2,1)S(1)}, bf16[2,1,64,2816]{3,2,0,1:T(8,128)(2,1)S(1)}, u32[]{:S(2)}, u32[]{:S(2)}) collective-permute-start(bf16[2,1,64,2816]{3,2,0,1:T(8,128)(2,1)S(1)} %pad_maximum_fusion.17), channel_id=1, source_target_pairs={{0,16},{4,20},{8,24},{12,28},{16,0},{20,4},{24,8},{28,12},{1,17},{... | collective-permute-start | bytes 2162696 | tf_op jit(solution)/shard_map/ppermute | solution.py:27
  118.9 32.6 %collective-permute-start.4 = (bf16[4,1,1,64,1664]{4,3,2,1,0:T(8,128)(2,1)S(1)}, bf16[4,1,1,64,1664]{4,3,2,1,0:T(8,128)(2,1)S(1)}, u32[]{:S(2)}, u32[]{:S(2)}) collective-permute-start(bf16[4,1,1,64,1664]{4,3,2,1,0:T(8,128)(2,1)S(1)} %maximum_bitcast_fusion.1), channel_id=1, source_target_pairs={{0,4},{4,0},{8,12},{12,8},{16,20},{20,16},{24,28},{28,24},{1,5},{5... | collective-permute-start | bytes 2555912 | tf_op jit(solution)/shard_map/ppermute | solution.py:27
  129.8 52.6 %collective-permute-start.26 = (bf16[4,1,1,64,2816]{4,3,2,1,0:T(8,128)(2,1)S(1)}, bf16[4,1,1,64,2816]{4,3,2,1,0:T(8,128)(2,1)S(1)}, u32[]{:S(2)}, u32[]{:S(2)}) collective-permute-start(bf16[4,1,1,64,2816]{4,3,2,1,0:T(8,128)(2,1)S(1)} %maximum_bitcast_fusion), channel_id=1, source_target_pairs={{0,4},{4,0},{8,12},{12,8},{16,20},{20,16},{24,28},{28,24},{1,5},{5... | collective-permute-start | bytes 4325384 | tf_op jit(solution)/shard_map/ppermute | solution.py:27
  133.3 31.5 %collective-permute-start.9 = (bf16[2,384,512]{2,1,0:T(8,128)(2,1)S(1)}, bf16[2,384,512]{2,1,0:T(8,128)(2,1)S(1)}, u32[]{:S(2)}, u32[]{:S(2)}) collective-permute-start(bf16[2,384,512]{2,1,0:T(8,128)(2,1)S(1)} %collective-permute-done.8.refs_5_.refs_10_), channel_id=1, source_target_pairs={{0,8},{4,12},{8,16},{12,20},{16,24},{20,28},{1,9},{5,13},{9,17},{1... | collective-permute-start | bytes 2359304 | tf_op jit(solution)/shard_map/ppermute | solution.py:448
  148.0 81.7 %collective-permute-start.12 = (bf16[2,384,512]{2,1,0:T(8,128)(2,1)S(1)}, bf16[2,384,512]{2,1,0:T(8,128)(2,1)S(1)}, u32[]{:S(2)}, u32[]{:S(2)}) collective-permute-start(bf16[2,384,512]{2,1,0:T(8,128)(2,1)S(1)} %collective-permute-done.8.refs_5_.refs_10_), channel_id=1, source_target_pairs={{0,4},{4,0},{8,12},{12,8},{16,20},{20,16},{24,28},{28,24},{1,5},{5... | collective-permute-start | bytes 2359304 | tf_op jit(solution)/shard_map/ppermute | solution.py:27
  151.6 34.5 %collective-permute-start.32 = (bf16[4,2,1,176,512]{4,3,2,1,0:T(8,128)(2,1)S(1)}, bf16[4,2,1,176,512]{4,3,2,1,0:T(8,128)(2,1)S(1)}, u32[]{:S(2)}, u32[]{:S(2)}) collective-permute-start(bf16[4,2,1,176,512]{4,3,2,1,0:T(8,128)(2,1)S(1)} %pad_maximum_fusion.8), channel_id=1, source_target_pairs={{0,2},{1,3},{2,0},{3,1},{4,6},{5,7},{6,4},{7,5},{8,10},{9,11},{10,... | collective-permute-start | bytes 4325384 | tf_op jit(solution)/shard_map/ppermute | solution.py:27
  164.8 57.8 %collective-permute-start.5 = (bf16[4,2,1,64,1664]{4,3,2,1,0:T(8,128)(2,1)S(1)}, bf16[4,2,1,64,1664]{4,3,2,1,0:T(8,128)(2,1)S(1)}, u32[]{:S(2)}, u32[]{:S(2)}) collective-permute-start(bf16[4,2,1,64,1664]{4,3,2,1,0:T(8,128)(2,1)S(1)} %pad_maximum_fusion.7), channel_id=1, source_target_pairs={{0,2},{1,3},{2,0},{3,1},{4,6},{5,7},{6,4},{7,5},{8,10},{9,11},{10,... | collective-permute-start | bytes 5111816 | tf_op jit(solution)/shard_map/ppermute | solution.py:27
  186.1 43.6 %collective-permute-start.13 = (bf16[2,384,512]{2,1,0:T(8,128)(2,1)S(1)}, bf16[2,384,512]{2,1,0:T(8,128)(2,1)S(1)}, u32[]{:S(2)}, u32[]{:S(2)}) collective-permute-start(bf16[2,384,512]{2,1,0:T(8,128)(2,1)S(1)} %collective-permute-done.9.refs_6_.refs_11_), channel_id=1, source_target_pairs={{0,4},{4,0},{8,12},{12,8},{16,20},{20,16},{24,28},{28,24},{1,5},{5... | collective-permute-start | bytes 2359304 | tf_op jit(solution)/shard_map/ppermute | solution.py:27
  198.8 83.2 %collective-permute-start.27 = (bf16[4,2,1,64,2816]{4,3,2,1,0:T(8,128)(2,1)}, bf16[4,2,1,64,2816]{4,3,2,1,0:T(8,128)(2,1)}, u32[]{:S(2)}, u32[]{:S(2)}) collective-permute-start(bf16[4,2,1,64,2816]{4,3,2,1,0:T(8,128)(2,1)} %pad_maximum_fusion.2), channel_id=1, source_target_pairs={{0,2},{1,3},{2,0},{3,1},{4,6},{5,7},{6,4},{7,5},{8,10},{9,11},{10,... | collective-permute-start | bytes 8650760 | tf_op jit(solution)/shard_map/ppermute | solution.py:27
  304.4 62.9 %collective-permute-start.49 = (bf16[4,2,64,1408]{3,2,1,0:T(8,128)(2,1)}, bf16[4,2,64,1408]{3,2,1,0:T(8,128)(2,1)}, u32[]{:S(2)}, u32[]{:S(2)}) collective-permute-start(bf16[4,2,64,1408]{3,2,1,0:T(8,128)(2,1)} %dynamic-slice_bitcast_fusion.3), channel_id=1, source_target_pairs={{0,4},{4,0},{8,12},{12,8},{16,20},{20,16},{24,28},{28,24},{1,5},{5... | collective-permute-start | bytes 4325384 | tf_op jit(solution)/shard_map/ppermute | solution.py:27
  306.2 92.8 %collective-permute-start.54 = (bf16[4,2,64,1408]{3,2,1,0:T(8,128)(2,1)}, bf16[4,2,64,1408]{3,2,1,0:T(8,128)(2,1)}, u32[]{:S(2)}, u32[]{:S(2)}) collective-permute-start(bf16[4,2,64,1408]{3,2,1,0:T(8,128)(2,1)} %dynamic-slice_bitcast_fusion.2), channel_id=1, source_target_pairs={{0,2},{1,3},{2,0},{3,1},{4,6},{5,7},{6,4},{7,5},{8,10},{9,11},{10,... | collective-permute-start | bytes 4325384 | tf_op jit(solution)/shard_map/ppermute | solution.py:27
  308.9 38.3 %collective-permute-start.59 = (bf16[384,1408]{1,0:T(8,128)(2,1)}, bf16[384,1408]{1,0:T(8,128)(2,1)}, u32[]{:S(2)}, u32[]{:S(2)}) collective-permute-start(bf16[384,1408]{1,0:T(8,128)(2,1)} %pad_maximum_fusion.9), channel_id=1, source_target_pairs={{0,1},{1,0},{2,3},{3,2},{4,5},{5,4},{6,7},{7,6},{8,9},{9,8},{10,11... | collective-permute-start | bytes 3244040 | tf_op jit(solution)/shard_map/ppermute | solution.py:27
  351.7 96.4 %collective-permute-start.60 = (bf16[4,2,176,512]{3,2,1,0:T(8,128)(2,1)}, bf16[4,2,176,512]{3,2,1,0:T(8,128)(2,1)}, u32[]{:S(2)}, u32[]{:S(2)}) collective-permute-start(bf16[4,2,176,512]{3,2,1,0:T(8,128)(2,1)} %dynamic-slice_bitcast_fusion.1), channel_id=1, source_target_pairs={{0,4},{4,0},{8,12},{12,8},{16,20},{20,16},{24,28},{28,24},{1,5},{5... | collective-permute-start | bytes 4325384 | tf_op jit(solution)/shard_map/ppermute | solution.py:27
  360.6 95.0 %collective-permute-start.38 = (bf16[4,2,64,1664]{3,2,1,0:T(8,128)(2,1)S(1)}, bf16[4,2,64,1664]{3,2,1,0:T(8,128)(2,1)S(1)}, u32[]{:S(2)}, u32[]{:S(2)}) collective-permute-start(bf16[4,2,64,1664]{3,2,1,0:T(8,128)(2,1)S(1)} %dynamic-slice_bitcast_fusion), channel_id=1, source_target_pairs={{0,2},{1,3},{2,0},{3,1},{4,6},{5,7},{6,4},{7,5},{8,10},{9,11},{10,... | collective-permute-start | bytes 5111816 | tf_op jit(solution)/shard_map/ppermute | solution.py:27
  456.2 30.4 %collective-permute-start.39 = (bf16[4,64,1664]{2,1,0:T(8,128)(2,1)S(1)}, bf16[4,64,1664]{2,1,0:T(8,128)(2,1)S(1)}, u32[]{:S(2)}, u32[]{:S(2)}) collective-permute-start(bf16[4,64,1664]{2,1,0:T(8,128)(2,1)S(1)} %dynamic-slice_bitcast_fusion.5), channel_id=1, source_target_pairs={{0,4},{4,0},{8,12},{12,8},{16,20},{20,16},{24,28},{28,24},{1,5},{5... | collective-permute-start | bytes 2555912 | tf_op jit(solution)/shard_map/ppermute | solution.py:27
  (98 other events, 1050.6 us)

commit v2 on v1

v2 whole, which is shorter than its diff:
```python
import jax
import jax.numpy as jnp
from jax import lax
from jax.experimental import pallas as pl
from jax.experimental.pallas import tpu as pltpu
from jax.sharding import PartitionSpec as P

H = 8
HD = 128
EPSILON = 1e-05
NEG_BIG = -1e30
POS_BIG = 1e30
ROPE_BASE = 10000.0
LANES = 128
KERNEL_HIGH = 2

BF = jnp.bfloat16
F32 = jnp.float32


def cdiv(a, b):
    return -(-a // b)


def flip(value, axis, bit):
    count = lax.axis_size(axis)
    return lax.ppermute(value, axis, [(i, i ^ bit) for i in range(count)])


def flip_core(value):
    return flip(value, "rep", 1)


def flip_y(value):
    return flip(value, "rep", 2)


def flip_x(value):
    return flip(value, "seg", 1)


def flip_z(value):
    return flip(value, "seg", 2)


def ordered(mine, other, bit, axis):
    first = jnp.where(bit == 0, mine, other)
    second = jnp.where(bit == 0, other, mine)
    return jnp.concatenate([first, second], axis)


def pick(value, index, axis):
    return lax.dynamic_index_in_dim(value, index, axis, keepdims=False)


def cut(value, start, size, axis=-1):
    return lax.dynamic_slice_in_dim(value, start, size, axis % value.ndim)


def fence(*values):
    return lax.optimization_barrier(values)


def place():
    seg = lax.axis_index("seg")
    rep = lax.axis_index("rep")
    return seg % 2, (seg // 2) % 2, seg // 4, rep // 2, rep % 2


def high_bits():
    bit = 4
    out = []
    while bit < lax.axis_size("seg"):
        out.append(bit)
        bit *= 2
    return out


def gather_high(cur):
    seg = lax.axis_index("seg")
    for bit in high_bits():
        cur = ordered(cur, flip(cur, "seg", bit), (seg // bit) % 2, 0)
    return cur


def gather_x(cur):
    return ordered(cur, flip_x(cur), place()[0], 2)


def gather_y(cur):
    return ordered(cur, flip_y(cur), place()[3], 3)


def flat(cur):
    return cur.reshape(-1, cur.shape[-1])


def halve(value, axis_name, bit, side, axis):
    recv = flip(pick(value, 1 - side, axis), axis_name, bit)
    kept = pick(value, side, axis)
    return (kept.astype(F32) + recv.astype(F32)).astype(BF)


def reduce_plane(full, low, x_first):
    x, unused, unused, y, unused = place()
    high = lax.axis_size("seg") // 4
    total, cols = full.shape
    cur = full.reshape(high, low, 2, 2, total // (high * low * 4), cols)
    if x_first:
        cur = halve(cur, "seg", 1, x, 2)
        return halve(cur, "rep", 2, y, 2)
    cur = halve(cur, "rep", 2, y, 3)
    return halve(cur, "seg", 1, x, 2)


def reduce_high(cur):
    seg = lax.axis_index("seg")
    for bit in reversed(high_bits()):
        cur = cur.reshape((2, cur.shape[0] // 2) + cur.shape[1:])
        cur = halve(cur, "seg", bit, (seg // bit) % 2, 0)
    return cur[0]


def trade_core(quarters):
    core = place()[4]
    low, unused, rows, cols = 2, 2, quarters.shape[1], quarters.shape[2]
    four = quarters.reshape(2, 2, rows, cols)
    return ordered(pick(four, core, 1), flip_core(pick(four, 1 - core, 1)), core, 1)


def trade_z(halves):
    low = place()[1]
    return ordered(pick(halves, low, 0)[None], flip_z(pick(halves, 1 - low, 0))[None], low, 0)


def gather_z_four(halves):
    seg = lax.axis_index("seg")
    low = (seg // 2) % 2
    keep, give = pick(halves, low, 0)[None, None], pick(halves, 1 - low, 0)[None, None]
    near = ordered(keep, flip(give, "seg", 2), low, 1)
    far = ordered(flip(keep, "seg", 4), flip(give, "seg", 6), low, 1)
    return ordered(near, far, (seg // 4) % 2, 0)[:, :, None, None]


def start_gather(traded):
    return traded[None, :, None, None]


def untrade(sums):
    unused, low, unused, unused, core = place()
    twice, cols = sums.shape[1:]
    mine = ordered(pick(sums, low, 0)[None], flip_z(pick(sums, 1 - low, 0))[None], low, 0)
    four = mine.reshape(2, 2, twice // 2, cols)
    kept = pick(four, core, 1)[:, None]
    return ordered(kept, flip_core(pick(four, 1 - core, 1))[:, None], core, 1)


def swap_pairs(value):
    blocks = value.reshape((value.shape[0], 2, 2, value.shape[1] // 4) + value.shape[2:])
    return jnp.stack([blocks[:, :, 1], blocks[:, :, 0]], 2).reshape(value.shape)


def all_quarters(mine, far, of_tokens):
    unused, low, unused, unused, core = place()
    other = flip_core(jnp.stack([mine, far]))
    if of_tokens:
        other = swap_pairs(other)
    near_half = ordered(mine, other[0], core, 1)
    far_half = ordered(far, other[1], core, 1)
    return ordered(near_half, far_half, low, 1)


def all_blocks(near_pair, far):
    low = place()[1]
    far_pair = jnp.stack([far, flip_core(far)])
    return ordered(near_pair, far_pair, low, 0)


def core_sums(part):
    blocks = part.reshape((2, 2, part.shape[0] // 4) + part.shape[1:])
    return (blocks[:, 0] + flip_core(blocks[:, 1].astype(BF)).astype(F32)).astype(BF)


def own_sums(sums):
    low = place()[1]
    return pick(sums, low, 0).astype(F32) + flip_z(pick(sums, 1 - low, 0)).astype(F32)


def all_sums(sums):
    both = (sums.astype(F32) + flip_z(sums).astype(F32)).astype(BF)
    return jnp.concatenate([both[:, None], flip_core(both)[:, None]], 1).astype(F32)


def unit_blocks(n_blocks):
    order = []
    for block in range(n_blocks):
        high, low, rest, core = block // 16, (block // 8) % 2, (block // 2) % 4, block % 2
        order.append((low * 2 + core, high * 4 + rest))
    return order


def split_units(matrix, n_blocks):
    rows, total = matrix.shape
    size = total // n_blocks

    def body(in_ref, out_ref):
        for block, (quarter, at) in enumerate(unit_blocks(n_blocks)):
            out_ref[quarter, :, at * size : (at + 1) * size] = in_ref[:, block * size : (block + 1) * size]

    return pl.pallas_call(
        body,
        out_shape=jax.ShapeDtypeStruct((4, rows, total // 4), matrix.dtype),
        name="split_units",
    )(matrix)


def join_units(quarters, n_blocks):
    unused, rows, quarter_size = quarters.shape
    size = 4 * quarter_size // n_blocks

    def body(in_ref, out_ref):
        for block, (quarter, at) in enumerate(unit_blocks(n_blocks)):
            out_ref[:, block * size : (block + 1) * size] = in_ref[
                quarter, :, at * size : (at + 1) * size
            ].astype(F32)

    return pl.pallas_call(
        body,
        out_shape=jax.ShapeDtypeStruct((rows, 4 * quarter_size), F32),
        name="join_units",
    )(quarters)


def matmul(left, right):
    return jnp.dot(left, right, preferred_element_type=F32)


def matmul_rows(left, right):
    return lax.dot_general(left, right, (((0,), (0,)), ((), ())), preferred_element_type=F32)


def matmul_cols(left, right):
    return lax.dot_general(left, right, (((1,), (1,)), ((), ())), preferred_element_type=F32)


def norm_forward(values, gain):
    inverse = lax.rsqrt(jnp.mean(values * values, axis=-1, keepdims=True) + EPSILON)
    return (values * inverse * gain, inverse)


def norm_backward(values, inverse, gain, grad_out):
    normed = values * inverse
    scaled = grad_out * gain
    grad_values = inverse * (scaled - normed * jnp.mean(scaled * normed, axis=-1, keepdims=True))
    return (grad_values, normed)


def rope_tables(seg_len):
    position = jnp.arange(seg_len).astype(F32)
    freqs = ROPE_BASE ** (-(2.0 * jnp.arange(HD // 2).astype(F32)) / HD)
    angle = position[:, None] * freqs[None, :]
    cosine, sine = jnp.cos(angle), jnp.sin(angle)
    return (jnp.concatenate([cosine, cosine], -1), jnp.concatenate([-sine, sine], -1))


def rope_heads(values, cosine, sine):
    half = HD // 2
    swapped = jnp.concatenate([values[..., half:], values[..., :half]], -1)
    return values * cosine[:, None, :] + swapped * sine[:, None, :]


def mask_kernel(n_cols, cols_ref, out_ref, scratch):
    queries = cols_ref.shape[1]
    picks = cols_ref[0]
    pad = scratch.shape[0]
    high = lax.shift_right_arithmetic(picks, 7)
    low = jnp.bitwise_and(picks, LANES - 1).astype(F32)
    rows = 16
    iota_high = lax.broadcasted_iota(jnp.int32, (pad, picks.shape[1]), 0)
    iota_low = lax.broadcasted_iota(jnp.int32, (rows, picks.shape[1]), 0).astype(F32).astype(BF)
    one, zero = jnp.ones_like(iota_low), jnp.zeros_like(iota_low)
    for i in range(queries):
        hot_high = jnp.where(iota_high == high[i : i + 1, :], 1.0, 0.0).astype(BF)
        wanted = jnp.broadcast_to(low[i : i + 1, :], iota_low.shape).astype(BF)
        hot_low = jnp.concatenate(
            [jnp.where(iota_low == wanted - float(first), one, zero) for first in range(0, LANES, rows)], 0
        )
        scratch[:, i, :] = matmul_cols(hot_high, hot_low)
    out_ref[0] = jnp.where(scratch[0:n_cols] > 0.5, POS_BIG, NEG_BIG).astype(BF)


def build_mask(columns, n_cols):
    rows, queries, picks = columns.shape
    block = 16
    pad = cdiv(n_cols, 8) * 8
    return pl.pallas_call(
        lambda *refs: mask_kernel(n_cols, *refs),
        grid=(rows, queries // block),
        in_specs=[pl.BlockSpec((1, block, picks), lambda r, g: (r, g, 0))],
        out_specs=pl.BlockSpec((1, n_cols, block, LANES), lambda r, g: (r, 0, g, 0)),
        out_shape=jax.ShapeDtypeStruct((rows, n_cols, queries, LANES), BF),
        scratch_shapes=[pltpu.VMEM((pad, block, LANES), F32)],
        compiler_params=pltpu.CompilerParams(vmem_limit_bytes=16 * 1024 * 1024),
        cost_estimate=pl.CostEstimate(
            flops=20 * rows * queries * pad * picks * LANES, bytes_accessed=5000000, transcendentals=0
        ),
        name="mask_build",
    )(columns)


def lane_blocks(value):
    return [value[:, i : i + LANES] for i in range(0, value.shape[1], LANES)]


PIECES = ((0, 0), (0, 1), (1, 0), (1, 1), (2, 0), (3, 0), (2, 1))
N_COMMON = 5
N_GROUPS = 4


def forward_kernel(q_ref, k_ref, v_ref, live_ref, mask_ref, *refs):
    key_refs, value_refs = refs[:N_GROUPS], refs[N_GROUPS : 2 * N_GROUPS]
    o_ref, of_ref, p_ref, pl_ref, inv_ref, s_ref, top_ref, total_ref, acc_ref = refs[2 * N_GROUPS :]
    scale = HD ** (-0.5)
    upper = pl.program_id(1) >= 2
    queries = q_ref[0]
    seg_len = queries.shape[0]
    row = lax.broadcasted_iota(jnp.int32, (seg_len, seg_len), 0)
    col = lax.broadcasted_iota(jnp.int32, (seg_len, seg_len), 1)
    allow = (col == row) | ((col < row) & (live_ref[0] == 1))
    s_local = jnp.where(allow, matmul_cols(queries, k_ref[0]) * scale, NEG_BIG)
    per = key_refs[0].shape[1] // LANES

    def score(t, top):
        group, low = PIECES[t]
        parts = lane_blocks(matmul_cols(queries, key_refs[group][low]) * scale)
        for i in range(per):
            part = jnp.minimum(parts[i], mask_ref[0, t * per + i].astype(F32))
            s_ref[t, :, i * LANES : (i + 1) * LANES] = part
            top = part if top is None else jnp.maximum(top, part)
        return top

    top = None
    for t in range(N_COMMON):
        top = score(t, top)
    top_ref[...] = top

    @pl.when(upper)
    def more_scores():
        more = top_ref[...]
        for t in range(N_COMMON, len(PIECES)):
            more = score(t, more)
        top_ref[...] = more

    row_max = jnp.maximum(
        jnp.max(s_local, axis=-1, keepdims=True), jnp.max(top_ref[...], axis=-1, keepdims=True)
    )
    e_local = jnp.exp(s_local - row_max)
    low_local = e_local.astype(BF)
    pl_ref[0, 0] = low_local

    def weigh(t, total, acc):
        group, low = PIECES[t]
        expo = jnp.exp(s_ref[t] - row_max)
        for part in lane_blocks(expo):
            total = part if total is None else total + part
        chances = expo.astype(BF)
        p_ref[0, 0, t] = chances
        return total, acc + matmul(chances, value_refs[group][low])

    total, acc = None, matmul(low_local, v_ref[0])
    for t in range(N_COMMON):
        total, acc = weigh(t, total, acc)
    total_ref[...] = total
    acc_ref[...] = acc

    @pl.when(upper)
    def more_values():
        total, acc = total_ref[...], acc_ref[...]
        for t in range(N_COMMON, len(PIECES)):
            total, acc = weigh(t, total, acc)
        total_ref[...] = total
        acc_ref[...] = acc

    row_total = jnp.sum(e_local, axis=-1, keepdims=True) + jnp.sum(total_ref[...], axis=-1, keepdims=True)
    inverse = 1.0 / row_total
    out = acc_ref[...] * inverse
    of_ref[0] = out
    o_ref[0] = out.astype(BF)
    inv_ref[0, 0] = inverse


def backward_local_kernel(do_ref, of_ref, q_ref, k_ref, v_ref, inv_ref, pl_ref, cos_ref, sin_ref, dkv_ref, dq_ref):
    scale = HD ** (-0.5)
    d_out = do_ref[0]
    delta = jnp.sum(d_out.astype(F32) * of_ref[0], axis=-1, keepdims=True)
    chances = pl_ref[0, 0].astype(F32) * inv_ref[0, 0]
    ds = (chances * (matmul_cols(d_out, v_ref[0]) - delta)).astype(BF)
    dq_ref[0] = matmul(ds, k_ref[0])
    dk = matmul_rows(ds, q_ref[0])
    dkv_ref[0, 0] = ((dk * cos_ref[...] - pltpu.roll(dk, HD // 2, 1) * sin_ref[...]) * scale).astype(BF)
    dkv_ref[1, 0] = matmul_rows(chances.astype(BF), d_out).astype(BF)


def backward_kernel(do_ref, of_ref, local_ref, inv_ref, p_ref, cos_ref, sin_ref, *refs):
    key_refs, value_refs = refs[:N_GROUPS], refs[N_GROUPS : 2 * N_GROUPS]
    out_ref, dq_ref = refs[2 * N_GROUPS :]
    scale = HD ** (-0.5)
    upper = pl.program_id(1) >= 2
    d_out = do_ref[0]
    inverse = inv_ref[0, 0]
    delta = jnp.sum(d_out.astype(F32) * of_ref[0], axis=-1, keepdims=True)

    def piece(t, dq):
        group, low = PIECES[t]
        dp = matmul_cols(d_out, value_refs[group][low])
        ds = (p_ref[0, 0, t].astype(F32) * ((dp - delta) * inverse)).astype(BF)
        return dq + matmul(ds, key_refs[group][low])

    dq = local_ref[0]
    for t in range(N_COMMON):
        dq = piece(t, dq)
    dq_ref[...] = dq

    @pl.when(upper)
    def more():
        dq = dq_ref[...]
        for t in range(N_COMMON, len(PIECES)):
            dq = piece(t, dq)
        dq_ref[...] = dq

    dq = dq_ref[...]
    out_ref[0] = ((dq * cos_ref[...] - pltpu.roll(dq, HD // 2, 1) * sin_ref[...]) * scale).astype(BF)


def attention_specs(piece_rows, seg_len):
    head = pl.BlockSpec((1, seg_len, HD), lambda h, r: (r, 0, h))
    piece = pl.BlockSpec((2, piece_rows, HD), lambda h, r: (0, 0, h))
    p_spec = pl.BlockSpec((1, 1, len(PIECES), seg_len, piece_rows), lambda h, r: (r, h, 0, 0, 0))
    pl_spec = pl.BlockSpec((1, 1, seg_len, seg_len), lambda h, r: (r, h, 0, 0))
    inv_spec = pl.BlockSpec((1, 1, seg_len, 1), lambda h, r: (r, h, 0, 0))
    return head, piece, p_spec, pl_spec, inv_spec


def attention_forward(queries, keys, values, live, mask, key_pieces, value_pieces):
    blocks, seg_len, width = queries.shape
    heads = width // HD
    piece_rows = key_pieces[0].shape[1]
    head, piece, p_spec, pl_spec, inv_spec = attention_specs(piece_rows, seg_len)
    flops = 4 * blocks * heads * seg_len * HD * (len(PIECES) * piece_rows + seg_len)
    return pl.pallas_call(
        forward_kernel,
        grid=(heads, blocks),
        in_specs=[
            head,
            head,
            head,
            pl.BlockSpec((1, 1, seg_len), lambda h, r: (r, 0, 0)),
            pl.BlockSpec((1,) + mask.shape[1:], lambda h, r: (r, 0, 0, 0)),
        ]
        + [piece] * (2 * N_GROUPS),
        out_specs=[head, head, p_spec, pl_spec, inv_spec],
        out_shape=[
            jax.ShapeDtypeStruct(queries.shape, BF),
            jax.ShapeDtypeStruct(queries.shape, F32),
            jax.ShapeDtypeStruct((blocks, heads, len(PIECES), seg_len, piece_rows), BF),
            jax.ShapeDtypeStruct((blocks, heads, seg_len, seg_len), BF),
            jax.ShapeDtypeStruct((blocks, heads, seg_len, 1), F32),
        ],
        scratch_shapes=[
            pltpu.VMEM((len(PIECES), seg_len, piece_rows), F32),
            pltpu.VMEM((seg_len, LANES), F32),
            pltpu.VMEM((seg_len, LANES), F32),
            pltpu.VMEM((seg_len, HD), F32),
        ],
        compiler_params=pltpu.CompilerParams(vmem_limit_bytes=40 * 1024 * 1024),
        cost_estimate=pl.CostEstimate(flops=8 * flops, bytes_accessed=20000000, transcendentals=flops // 512),
        name="attention_forward",
    )(queries, keys, values, live, mask, *key_pieces, *value_pieces)


def attention_backward_local(d_out, out_f32, queries, keys, values, inverse, p_local, cosine, sine):
    blocks, seg_len, width = queries.shape
    head, unused, unused, pl_spec, inv_spec = attention_specs(seg_len, seg_len)
    table = pl.BlockSpec((seg_len, HD), lambda h, r: (0, 0))
    return pl.pallas_call(
        backward_local_kernel,
        grid=(width // HD, blocks),
        in_specs=[head, head, head, head, head, inv_spec, pl_spec, table, table],
        out_specs=[pl.BlockSpec((2, 1, seg_len, HD), lambda h, r: (0, r, 0, h)), head],
        out_shape=[
            jax.ShapeDtypeStruct((2, blocks, seg_len, width), BF),
            jax.ShapeDtypeStruct(queries.shape, F32),
        ],
        compiler_params=pltpu.CompilerParams(vmem_limit_bytes=16 * 1024 * 1024),
        cost_estimate=pl.CostEstimate(flops=3000000000, bytes_accessed=5000000, transcendentals=0),
        name="attention_backward_local",
    )(d_out, out_f32, queries, keys, values, inverse, p_local, cosine, sine)


def attention_backward(d_out, out_f32, dq_local, inverse, p_memory, cosine, sine, key_pieces, value_pieces):
    blocks, seg_len, width = d_out.shape
    heads = width // HD
    piece_rows = key_pieces[0].shape[1]
    head, piece, p_spec, unused, inv_spec = attention_specs(piece_rows, seg_len)
    table = pl.BlockSpec((seg_len, HD), lambda h, r: (0, 0))
    flops = 4 * blocks * heads * seg_len * HD * len(PIECES) * piece_rows
    return pl.pallas_call(
        backward_kernel,
        grid=(heads, blocks),
        in_specs=[head, head, head, inv_spec, p_spec, table, table] + [piece] * (2 * N_GROUPS),
        out_specs=head,
        out_shape=jax.ShapeDtypeStruct((blocks, seg_len, width), BF),
        scratch_shapes=[pltpu.VMEM((seg_len, HD), F32)],
        compiler_params=pltpu.CompilerParams(vmem_limit_bytes=40 * 1024 * 1024),
        cost_estimate=pl.CostEstimate(flops=8 * flops, bytes_accessed=20000000, transcendentals=0),
        name="attention_backward",
    )(d_out, out_f32, dq_local, inverse, p_memory, cosine, sine, *key_pieces, *value_pieces)


def allow_local_of(live):
    seg_len = live.shape[-1]
    position = jnp.arange(seg_len, dtype=jnp.int32)
    same = position[None, :] == position[:, None]
    return same[None] | ((position[None, :] < position[:, None])[None] & (live == 1))


def split_heads(value):
    rows, seg_len, width = value.shape
    return value.reshape(rows, seg_len, width // HD, HD)


def stream_forward(queries, keys, values, live, allow, memory):
    scale = HD ** (-0.5)
    q4, k4, v4 = split_heads(queries), split_heads(keys), split_heads(values)
    scores = jnp.einsum("rqhd,rkhd->rhqk", q4, k4, preferred_element_type=F32) * scale
    scores = jnp.where(allow_local_of(live)[:, None], scores, NEG_BIG)
    row_max = jnp.max(scores, axis=-1)
    expo = jnp.exp(scores - row_max[..., None])
    state = (
        row_max,
        jnp.sum(expo, axis=-1),
        jnp.einsum("rhqk,rkhd->rhqd", expo.astype(BF), v4, preferred_element_type=F32),
    )

    def step(running, item):
        row_max, row_total, acc = running
        block, allowed = item
        k3 = block[0].reshape(block.shape[1], -1, HD)
        v3 = block[1].reshape(block.shape[1], -1, HD)
        scores = jnp.einsum("rqhd,khd->rhqk", q4, k3, preferred_element_type=F32) * scale
        scores = jnp.where(allowed[:, None] > 0, scores, NEG_BIG)
        new_max = jnp.maximum(row_max, jnp.max(scores, axis=-1))
        shrink = jnp.exp(row_max - new_max)
        expo = jnp.exp(scores - new_max[..., None])
        acc = acc * shrink[..., None] + jnp.einsum(
            "rhqk,khd->rhqd", expo.astype(BF), v3, preferred_element_type=F32
        )
        return (new_max, row_total * shrink + jnp.sum(expo, axis=-1), acc), None

    (row_max, row_total, acc), unused = lax.scan(step, state, (memory, allow))
    out = (acc / row_total[..., None]).transpose(0, 2, 1, 3).reshape(queries.shape)
    return out.astype(BF), out, row_max + jnp.log(row_total)


def stream_backward(d_out, out_f32, queries, keys, values, live, log_total, allow, memory, cosine, sine):
    scale = HD ** (-0.5)
    q4, k4, v4, d4 = split_heads(queries), split_heads(keys), split_heads(values), split_heads(d_out)
    delta = jnp.sum(d4.astype(F32) * split_heads(out_f32), axis=-1).transpose(0, 2, 1)
    scores = jnp.einsum("rqhd,rkhd->rhqk", q4, k4, preferred_element_type=F32) * scale
    scores = jnp.where(allow_local_of(live)[:, None], scores, NEG_BIG)
    chances = jnp.exp(scores - log_total[..., None])
    dp = jnp.einsum("rqhd,rkhd->rhqk", d4, v4, preferred_element_type=F32)
    ds = (chances * (dp - delta[..., None])).astype(BF)
    dq = jnp.einsum("rhqk,rkhd->rqhd", ds, k4, preferred_element_type=F32)
    dk = jnp.einsum("rhqk,rqhd->rkhd", ds, q4, preferred_element_type=F32)
    dv = jnp.einsum("rhqk,rqhd->rkhd", chances.astype(BF), d4, preferred_element_type=F32)

    def step(running, item):
        block, allowed = item
        k3 = block[0].reshape(block.shape[1], -1, HD)
        v3 = block[1].reshape(block.shape[1], -1, HD)
        scores = jnp.einsum("rqhd,khd->rhqk", q4, k3, preferred_element_type=F32) * scale
        scores = jnp.where(allowed[:, None] > 0, scores, NEG_BIG)
        chances = jnp.exp(scores - log_total[..., None])
        dp = jnp.einsum("rqhd,khd->rhqk", d4, v3, preferred_element_type=F32)
        ds = (chances * (dp - delta[..., None])).astype(BF)
        return running + jnp.einsum("rhqk,khd->rqhd", ds, k3, preferred_element_type=F32), None

    dq, unused = lax.scan(step, dq, (memory, allow))

    def back(value):
        turned = rope_heads(value.reshape((-1,) + value.shape[2:]), jnp.tile(cosine, (value.shape[0], 1)), -jnp.tile(sine, (value.shape[0], 1)))
        return (turned * scale).reshape(queries.shape).astype(BF)

    return jnp.stack([back(dq), back(dk), dv.reshape(queries.shape).astype(BF)])


def local(
    layer_input,
    live,
    knn_index,
    mem_keys,
    mem_values,
    gain_attn,
    w_query,
    w_key,
    w_value,
    w_out,
    gain_ffn,
    w_gate,
    w_up,
    w_down,
    cotangent,
):
    seg_len, width = layer_input.shape[1:]
    quarter = width // 4
    n_seg = lax.axis_size("seg")
    n_devices = n_seg * lax.axis_size("rep")
    tokens = seg_len * n_seg
    n_high = n_seg // 4
    x, low, high, y, core = place()
    use_kernel = n_high <= KERNEL_HIGH
    kv_rows = 2 * seg_len
    group_tokens = 4 * seg_len

    def by_quarter(value):
        return [value[:, i * quarter : (i + 1) * quarter] for i in range(4)]

    gains = jnp.concatenate(
        [gain_attn[:, None], gain_ffn[:, None], jnp.zeros((gain_attn.shape[0], LANES - 2), BF)], 1
    )
    stacked = [by_quarter(w) for w in (w_query, w_key, w_value, w_out)]
    qo = jnp.stack([jnp.concatenate([s[i] for s in stacked] + [gains], 1) for i in range(4)])

    def core_quarters(value, side):
        return jnp.stack([cut(value, side * quarter, quarter), cut(value, (2 + side) * quarter, quarter)])

    def core_memory(side):
        return jnp.stack([core_quarters(mem_keys[0], side), core_quarters(mem_values[0], side)])

    coded = knn_index[0] * 2 + live[0][:, None]
    kv = jnp.concatenate([core_memory(core), flip_core(core_memory(1 - core))], 2)
    qo = trade_core(qo)
    coded_pair = jnp.stack([coded, flip_core(coded)])
    qo, kv, coded, coded_pair = fence(qo, kv, coded, coded_pair)
    x_own, w_gate, w_up = layer_input[0], w_gate, w_up
    x_own, w_gate, w_up, qo = fence(x_own, w_gate, w_up, qo)

    kv_near, kv_far = pick(kv, low, 1), flip_z(pick(kv, 1 - low, 1))
    pieces = ordered(kv_near[:, None], kv_far[:, None], low, 1)
    own_k, own_v = pieces[0], pieces[1]
    coded_far = flip_z(coded)
    if use_kernel:
        qo = gather_z_four(qo)
    else:
        qo = gather_high(start_gather(trade_z(qo).reshape(2, -1, qo.shape[-1])))
    x_pair = jnp.stack([x_own, flip_core(x_own)])
    gate = split_units(w_gate, n_devices)
    upw = split_units(w_up, n_devices)
    qo, own_k, own_v, coded_far, x_pair, gate, upw = fence(qo, own_k, own_v, coded_far, x_pair, gate, upw)

    coded = all_blocks(coded_pair, coded_far)
    live_all = jnp.bitwise_and(coded[:, :, 0], 1)[:, None, :]
    picks = lax.shift_right_arithmetic(coded, 1)
    pair = picks >= tokens
    slot = jnp.where(pair, picks - tokens, picks)
    slot_seg = slot // seg_len
    swapped = (jnp.arange(4, dtype=jnp.int32) % 2)[:, None, None]
    kv_row = jnp.bitwise_xor(pair.astype(jnp.int32), swapped)
    within = kv_row * seg_len + (slot - slot_seg * seg_len)

    split = 2 * quarter
    x_far = flip_z(x_pair[0])
    gate = trade_core(gate)
    upw = trade_core(upw)

    def trade_rows(value):
        return start_gather(trade_z(value).reshape(2, -1, value.shape[-1]))

    down_w = w_down[None, None, None, None]
    if use_kernel:
        slot_x, slot_low = slot_seg % 2, (slot_seg // 2) % 2
        same_x = slot_x == x
        in_group = jnp.where(same_x, 5, 4 + 2 * slot_low)
        before = jnp.where(same_x, 0, 2) + slot_low
        piece_no = jnp.where(slot_seg // 4 == high, in_group, before)
        columns = jnp.where(picks >= 0, piece_no * kv_rows + within, -1)
        mask = build_mask(columns, len(PIECES) * kv_rows // LANES)
        up_high = [(i, i + 4) for i in range(n_seg - 4)]

        def cross(value):
            return lax.ppermute(value, "seg", up_high)

        cross_k = cross(own_k)
        side_k = flip_x(own_k)
        qo_a, qo_b = gather_x(qo[..., :split]), gather_y(qo[..., split:])
        qo_a, qo_b, cross_k, side_k, own_v, x_far, gate, upw, down_w = fence(
            qo_a, qo_b, cross_k, side_k, own_v, x_far, gate, upw, down_w
        )
        cross_v = cross(own_v)
        cross_side_k = flip_x(cross_k)
        qo_a, qo_b = gather_y(qo_a), gather_x(qo_b)
        gate, upw = trade_rows(gate), trade_rows(upw)
        down_w = gather_high(down_w)
        x_all = all_blocks(x_pair, x_far)
        qo_a, qo_b, cross_v, cross_side_k, own_v, gate, upw, down_w, x_all = fence(
            qo_a, qo_b, cross_v, cross_side_k, own_v, gate, upw, down_w, x_all
        )
        cross_side_v = flip_x(cross_v)
        side_v = flip_x(own_v)
        key_pieces = (cross_k, cross_side_k, side_k, own_k)
    else:
        qo_a, qo_b = gather_y(gather_x(qo[..., :split])), gather_x(gather_y(qo[..., split:]))
        x_all = all_blocks(x_pair, x_far)
        gate, upw = trade_rows(gate), trade_rows(upw)
        down_w = gather_high(down_w)
        columns = jnp.where(picks >= 0, slot_seg * kv_rows + within, n_seg * kv_rows)
        blocks_at = jnp.arange(4)[:, None, None]
        queries_at = jnp.arange(seg_len)[None, :, None]
        allow = jnp.zeros((4, seg_len, n_seg * kv_rows), BF).at[blocks_at, queries_at, columns].set(1.0, mode="drop")
        allow = allow.reshape(4, seg_len, n_seg, kv_rows).transpose(2, 0, 1, 3)
        memory = jnp.stack([own_k, own_v], 1)[None, :, None]
        memory = gather_x(gather_high(memory)).reshape(n_seg, 2, kv_rows, quarter)

    w_a, w_b = flat(qo_a), flat(qo_b)
    wo_near = w_b[:, quarter : 2 * quarter]
    g_attn = w_b[:, 2 * quarter].astype(F32)
    g_ffn = w_b[:, 2 * quarter + 1].astype(F32)
    gate = gather_high(gate)
    upw = gather_high(upw)

    x_float = x_all.reshape(group_tokens, width).astype(F32)
    cosine, sine = rope_tables(seg_len)
    cos_all = jnp.tile(cosine, (4, 1))
    sin_all = jnp.tile(sine, (4, 1))
    h_float, inv_one = norm_forward(x_float, g_attn)
    h_one = h_float.astype(BF)
    turned = rope_heads(matmul(h_one, w_a).reshape(group_tokens, -1, HD), cos_all, sin_all)
    turned = turned.reshape(group_tokens, 2 * quarter).astype(BF)
    w_v = w_b[:, :quarter]
    queries = turned[:, :quarter].reshape(4, seg_len, quarter)
    keys = turned[:, quarter:].reshape(4, seg_len, quarter)
    values = matmul(h_one, w_v).astype(BF).reshape(4, seg_len, quarter)
    if use_kernel:
        queries, keys, values, cross_side_v, side_v, gate, upw, down_w, wo_near = fence(
            queries, keys, values, cross_side_v, side_v, gate, upw, down_w, wo_near
        )
        value_pieces = (cross_v, cross_side_v, side_v, own_v)
        out_low, out_f32, p_memory, p_local, inverse = attention_forward(
            queries, keys, values, live_all, mask, key_pieces, value_pieces
        )
    else:
        out_low, out_f32, log_total = stream_forward(queries, keys, values, live_all, allow, memory)
    wo_far = flip_z(wo_near)
    gate, upw = gather_x(gate), gather_y(upw)
    down_w = gather_x(down_w)
    g_own = cotangent[0]
    out_low, wo_far, gate, upw, down_w, g_own = fence(out_low, wo_far, gate, upw, down_w, g_own)

    att_near = out_low.reshape(group_tokens, quarter)
    att_far = flip_z(att_near)
    gate, upw = gather_y(gate), gather_x(upw)
    wo = all_quarters(wo_near, wo_far, False)
    g_pair = jnp.stack([g_own, flip_core(g_own)])
    att_near, att_far, gate, upw, down_w, wo, g_own = fence(att_near, att_far, gate, upw, down_w, wo, g_own)

    wg, wu = flat(gate), flat(upw)
    wd = flat(gather_y(down_w))
    g_far = flip_z(g_own)
    attended = all_quarters(att_near, att_far, True)
    x_one = x_float + matmul(attended, wo)
    h_two_f, inv_two = norm_forward(x_one, g_ffn)
    h_two = h_two_f.astype(BF)
    gate_out = matmul(h_two, wg)
    up_out = matmul(h_two, wu)
    sigma = jax.nn.sigmoid(gate_out)
    swish = gate_out * sigma
    hidden = (swish * up_out).astype(BF)
    grad_out = all_blocks(g_pair, g_far).reshape(group_tokens, width)

    d_hidden = matmul_cols(grad_out, wd)
    d_gate = (d_hidden * up_out * sigma * (1.0 + gate_out * (1.0 - sigma))).astype(BF)
    d_up = (d_hidden * swish).astype(BF)
    sums = core_sums(matmul_cols(d_gate, wg) + matmul_cols(d_up, wu))
    sums, hidden, h_two, d_gate, d_up, wd = fence(sums, hidden, h_two, d_gate, d_up, wd)

    d_h_two = all_sums(sums).reshape(group_tokens, width)
    plane_wg = reduce_plane(matmul_rows(h_two, d_gate).astype(BF), 2, True)
    plane_wu = reduce_plane(matmul_rows(h_two, d_up).astype(BF), 2, False)
    grad_wd = matmul_rows(hidden, grad_out).astype(BF)
    down_sums = core_sums(matmul(hidden, wd))
    d_h_two, plane_wg, plane_wu, down_sums, grad_wd = fence(d_h_two, plane_wg, plane_wu, down_sums, grad_wd)

    own = 2 * low * seg_len
    d_x_norm, normed_two = norm_backward(x_one, inv_two, g_ffn, d_h_two)
    d_x_one = grad_out.astype(F32) + d_x_norm
    d_branch = d_x_one.astype(BF)
    grad_g_ffn = jnp.sum(cut(d_h_two, own, seg_len, 0) * cut(normed_two, own, seg_len, 0), axis=0)
    at_quarter = (2 * low + core) * quarter
    d_att = matmul_cols(d_branch, cut(wo, at_quarter, quarter, 0)).astype(BF).reshape(4, seg_len, quarter)
    plane_wd = reduce_plane(grad_wd, 1, True)
    high_wg = reduce_high(plane_wg)
    high_wu = reduce_high(plane_wu)
    layer_output = (cut(x_one, own, seg_len, 0) + own_sums(down_sums)).astype(BF)

    if use_kernel:
        d_kv, dq_local = attention_backward_local(
            d_att, out_f32, queries, keys, values, inverse, p_local, cosine, sine
        )
        d_kv, dq_local, d_att, d_branch, plane_wd, high_wg, high_wu, layer_output = fence(
            d_kv, dq_local, d_att, d_branch, plane_wd, high_wg, high_wu, layer_output
        )
    else:
        d_qkv = stream_backward(
            d_att, out_f32, queries, keys, values, live_all, log_total, allow, memory, cosine, sine
        )
        d_kv, d_q = d_qkv[1:], d_qkv[0]
    d_kv = d_kv.reshape(2, group_tokens, quarter)
    grad_kv = jnp.concatenate([matmul_rows(h_one, d_kv[i]).astype(BF) for i in range(2)], 1)
    grad_wo = matmul_rows(attended, cut(d_branch, at_quarter, quarter)).astype(BF)
    if use_kernel:
        d_att, grad_kv, grad_wo, dq_local = fence(d_att, grad_kv, grad_wo, dq_local)
        d_q = attention_backward(
            d_att, out_f32, dq_local, inverse, p_memory, cosine, sine, key_pieces, value_pieces
        )
    plane_kv = reduce_plane(grad_kv, 2, True)
    plane_wo = reduce_plane(grad_wo, 2, False)
    high_wd = reduce_high(plane_wd)
    four_wg = untrade(high_wg)
    four_wu = untrade(high_wu)
    d_q, plane_kv, plane_wo, high_wd, four_wg, four_wu = fence(d_q, plane_kv, plane_wo, high_wd, four_wg, four_wu)

    d_q = d_q.reshape(group_tokens, quarter)
    d_h_part = (
        matmul_cols(d_q, w_a[:, :quarter]) + matmul_cols(d_kv[0], w_a[:, quarter:]) + matmul_cols(d_kv[1], w_v)
    )
    grad_g_attn = jnp.sum(d_h_part * (x_float * inv_one), axis=0)
    d_h_sums = core_sums(d_h_part)
    grad_q = matmul_rows(h_one, d_q).astype(BF)
    grad_gains = jnp.concatenate(
        [
            grad_g_attn.astype(BF)[:, None],
            grad_g_ffn.astype(BF)[:, None],
            jnp.zeros((width, LANES - 2), BF),
        ],
        1,
    )
    plane_q = reduce_plane(jnp.concatenate([grad_q, grad_gains], 1), 2, False)
    high_kvo = reduce_high(jnp.concatenate([plane_kv, plane_wo], -1))
    d_h_one = own_sums(d_h_sums)
    x_own = cut(x_float, own, seg_len, 0)
    d_x_first, unused = norm_backward(x_own, cut(inv_one, own, seg_len, 0), g_attn, d_h_one)
    grad_x = (cut(d_x_one, own, seg_len, 0) + d_x_first).astype(BF)

    sum_wd = high_wd[0].astype(F32)
    sum_wg = join_units(four_wg.reshape(4, -1, high_wg.shape[-1]), n_devices)
    sum_wu = join_units(four_wu.reshape(4, -1, high_wu.shape[-1]), n_devices)
    sums = untrade(jnp.concatenate([reduce_high(plane_q), high_kvo], -1))
    sums = sums.reshape(4, -1, sums.shape[-1]).astype(F32)
    after = quarter + LANES

    def columns_of(at):
        return jnp.concatenate([sums[i][:, at : at + quarter] for i in range(4)], 1)

    sum_gains = jnp.sum(sums[:, :, quarter : quarter + 2], axis=0)
    return (
        layer_output[None],
        grad_x[None],
        sum_gains[:, 0],
        columns_of(0),
        columns_of(after),
        columns_of(after + quarter),
        columns_of(after + 2 * quarter),
        sum_gains[:, 1],
        sum_wg,
        sum_wu,
        sum_wd,
    )


def solution(mesh):
    tokens = P("rep", "seg", None)
    vector = P(("seg", "rep"))
    matrix = P(("seg", "rep"), None)
    return jax.shard_map(
        local,
        mesh=mesh,
        in_specs=(
            tokens,
            P("rep", "seg"),
            tokens,
            tokens,
            tokens,
            vector,
            matrix,
            matrix,
            matrix,
            matrix,
            vector,
            matrix,
            matrix,
            matrix,
            tokens,
        ),
        out_specs=(tokens, tokens, vector, matrix, matrix, matrix, matrix, vector, matrix, matrix, matrix),
        check_vma=False,
    )
```

time: 526 us -> 422 us (0.80)
  waiting for transfers between devices: 277 us -> 125 us
  local copies, waits for them, and re-layouts: 31.9 us -> 56.5 us
  Pallas kernels: 41.7 us -> 59.8 us
    ppermute x61 -> x70, waiting for transfers between devices: 255 us -> 125 us  [flip(): return lax.ppermute(value, axis, [(i, i ^ bit) for i in range(count)])]
    ppermute x4 -> x2, waiting for transfers between devices: 21.9 us -> 0.01 us  [cross(): return lax.ppermute(value, 'seg', up_high)]
    ppermute x61 -> x70, starting transfers between devices: 57.3 us -> 72.1 us  [flip(): return lax.ppermute(value, axis, [(i, i ^ bit) for i in range(count)])]
    ppermute x4 -> x2, starting transfers between devices: 20.7 us -> 6.41 us  [cross(): return lax.ppermute(value, 'seg', up_high)]
    pallas_call x1, Pallas kernels: 10.6 us -> 21.3 us  [build_mask(): pl.pallas_call(lambda *refs: mask_kernel(n_cols, *refs), grid=(rows, quer...]
    unnamed x118 -> x176, local copies, waits for them, and re-layouts: 5.69 us -> 15.6 us
    pallas_call x2 -> x7, Pallas kernels: 31 us -> 38.4 us  [the longest x1 13.4 us: attention_forward(): pl.pallas_call(forward_kernel, grid=(heads, blocks), in_specs=[head, head...]
    convert_element_type x2 -> x9, local copies, waits for them, and re-layouts: 2.29 us -> 9.06 us  [the longest x3 2.64 us: core_sums(): blocks[:, 1].astype(BF)]
  transfers between devices with their start and end apart: 65 -> 72, of which waited for: 32 -> 32; matrix products, arithmetic and copies ran while one was open for 18% -> 19% of each run, Pallas kernels for 8% -> 14%
where the time goes in v2:
time: 422 us; the launch traced here: 415 us
  waiting for transfers between devices  125 us (30%)
  starting transfers between devices  78.5 us (19%)
  Pallas kernels  59.8 us (14%)
  local copies, waits for them, and re-layouts  56.5 us (13%)
  other arithmetic  56.2 us (13%)
  matrix products  35 us (8%)
    ppermute x70, waiting for transfers between devices, flip(): return lax.ppermute(value, axis, [(i, i ^ bit) for i in range(count)])  125 us
    ppermute x70, starting transfers between devices, flip(): return lax.ppermute(value, axis, [(i, i ^ bit) for i in range(count)])  72.1 us
    pallas_call x1, Pallas kernels, build_mask(): pl.pallas_call(lambda *refs: mask_kernel(n_cols, *refs), grid=(rows, quer...  21.3 us
    unnamed x176, local copies, waits for them, and re-layouts  15.6 us
    dot_general x7, matrix products, matmul_cols(): lax.dot_general(left, right, (((1,), (1,)), ((), ())), preferred_element_...  13.5 us
    pallas_call x1, Pallas kernels, attention_forward(): pl.pallas_call(forward_kernel, grid=(heads, blocks), in_specs=[head, head...  13.4 us
    pallas_call x1, Pallas kernels, attention_backward(): pl.pallas_call(backward_kernel, grid=(heads, blocks), in_specs=[head, hea...  12.5 us
    dot_general x6, matrix products, matmul(): return jnp.dot(left, right, preferred_element_type=F32)  11.2 us
  transfers between devices with their start and end apart: 72, of which 32 were waited for; matrix products, arithmetic and copies ran while one was open for 19% of the time, Pallas kernels for 14%

profile of v2, /device:TPU:0, one launch (start us, length us, event | category | flops | bytes accessed | tf_op | source)
XLA Modules:
  0.0 414.6 jit_solution(14581347999454270157)
XLA Ops:
  22.3 11.1 %collective-permute-done.4 = bf16[1,1,64,1152]{3,2,1,0:T(8,128)(2,1)S(1)} collective-permute-done((bf16[1,1,64,1152]{3,2,1,0:T(8,128)(2,1)S(1)}, bf16[1,1,64,1152]{3,2,1,0:T(8,128)(2,1)S(1)}, u32[]{:S(2)}, u32[]{:S(2)}) %collective-permute-start.4) | collective-permute-done | bytes 147488 | tf_op jit(solution)/shard_map/ppermute | solution.py:27
  37.0 4.6 %collective-permute-start.11 = (bf16[2,384,256]{2,1,0:T(8,128)(2,1)S(1)}, bf16[2,384,256]{2,1,0:T(8,128)(2,1)S(1)}, u32[]{:S(2)}, u32[]{:S(2)}) collective-permute-start(bf16[2,384,256]{2,1,0:T(8,128)(2,1)S(1)} %get-tuple-element.110.refs_3_), channel_id=1, source_target_pairs={{0,16},{4,20},{8,24},{12,28},{1,17},{5,21},{9,25},{13,29},{2,18},{... | collective-permute-start | bytes 1179656 | tf_op jit(solution)/shard_map/ppermute | solution.py:692
  55.0 21.3 %mask_build.1.mask_ref = bf16[4,21,192,128]{3,2,1,0:T(8,128)(2,1)S(1)} custom-call(s32[4,192,128]{2,1,0:T(8,128)S(1)} %copy.214.refs_0_), custom_call_target="tpu_custom_call" | custom-call | flops 6039797760 | bytes 5000000 | tf_op jit(solution)/shard_map/mask_build/pallas_call | solution.py:296
  86.6 9.0 %collective-permute-done.20 = bf16[64,704]{1,0:T(8,128)(2,1)S(1)} collective-permute-done((bf16[64,704]{1,0:T(8,128)(2,1)S(1)}, bf16[64,704]{1,0:T(8,128)(2,1)S(1)}, u32[]{:S(2)}, u32[]{:S(2)}) %collective-permute-start.20) | collective-permute-done | bytes 90144 | tf_op jit(solution)/shard_map/ppermute | solution.py:27
  98.5 6.0 %collective-permute-done.22 = bf16[1,1,1,1,88,1024]{5,4,3,2,1,0:T(8,128)(2,1)S(1)} collective-permute-done((bf16[1,1,1,1,88,1024]{5,4,3,2,1,0:T(8,128)(2,1)S(1)}, bf16[1,1,1,1,88,1024]{5,4,3,2,1,0:T(8,128)(2,1)S(1)}, u32[]{:S(2)}, u32[]{:S(2)}) %collective-permute-start.22) | collective-permute-done | bytes 180256 | tf_op jit(solution)/shard_map/ppermute | solution.py:27
  108.7 3.5 collective-permute-done.19.refs_1_
  141.7 14.2 %collective-permute-start.29 = (bf16[1024,256]{1,0:T(8,128)(2,1)S(1)}, bf16[1024,256]{1,0:T(8,128)(2,1)S(1)}, u32[]{:S(2)}, u32[]{:S(2)}) collective-permute-start(bf16[1024,256]{1,0:T(8,128)(2,1)S(1)} %copy-done.33), channel_id=1, source_target_pairs={{0,8},{4,12},{8,0},{12,4},{16,24},{20,28},{24,16},{28,20},{1,9},{5... | collective-permute-start | bytes 1572872 | tf_op jit(solution)/shard_map/ppermute | solution.py:27
  159.4 13.4 %attention_forward.1 = (bf16[4,192,256]{2,1,0:T(8,128)(2,1)S(1)}, f32[4,192,256]{2,1,0:T(8,128)S(1)}, bf16[4,2,7,192,384]{4,3,2,1,0:T(8,128)(2,1)}, bf16[4,2,192...) custom-call(bf16[4,192,256]{2,1,0:T(8,128)(2,1)S(1)} %bitcast.372, bf16[4,192,256]{2,1,0:T(8,128)(2,1)S(1)} %bitcast.374, ...), custom_call_target="tpu_custom_call" | custom-call | flops 18119393280 | bytes 20000000 | tf_op jit(solution)/shard_map/attention_forward/pallas_call | solution.py:450
  176.0 15.2 %collective-permute-done.35 = bf16[2,2,2,1,64,704]{5,4,1,3,2,0:T(8,128)(2,1)S(1)} collective-permute-done((bf16[2,2,2,1,64,704]{5,4,1,3,2,0:T(8,128)(2,1)S(1)}, bf16[2,2,2,1,64,704]{5,4,1,3,2,0:T(8,128)(2,1)S(1)}, u32[]{:S(2)}, u32[]{:S(2)}) %collective-permute-start.35) | collective-permute-done | bytes 720928 | tf_op jit(solution)/shard_map/ppermute | solution.py:27
  195.5 6.5 %collective-permute-done.38 = bf16[192,1024]{1,0:T(8,128)(2,1)S(1)} collective-permute-done((bf16[192,1024]{1,0:T(8,128)(2,1)S(1)}, bf16[192,1024]{1,0:T(8,128)(2,1)S(1)}, u32[]{:S(2)}, u32[]{:S(2)}) %collective-permute-start.38) | collective-permute-done | bytes 393248 | tf_op jit(solution)/shard_map/ppermute | solution.py:27
  202.0 5.0 %collective-permute-done.41 = bf16[2,1,2,1,88,1024]{5,4,3,2,1,0:T(8,128)(2,1)S(1)} collective-permute-done((bf16[2,1,2,1,88,1024]{5,4,3,2,1,0:T(8,128)(2,1)S(1)}, bf16[2,1,2,1,88,1024]{5,4,3,2,1,0:T(8,128)(2,1)S(1)}, u32[]{:S(2)}, u32[]{:S(2)}) %collective-permute-start.41) | collective-permute-done | bytes 720928 | tf_op jit(solution)/shard_map/ppermute | solution.py:27
  227.2 3.5 convert.111
  255.7 7.2 %collective-permute-done.45 = bf16[2,2,2,64,704]{4,3,1,0,2:T(8,128)(2,1)} collective-permute-done((bf16[2,2,2,64,704]{4,3,1,0,2:T(8,128)(2,1)}, bf16[2,2,2,64,704]{4,3,1,0,2:T(8,128)(2,1)}, u32[]{:S(2)}, u32[]{:S(2)}) %collective-permute-start.45) | collective-permute-done | bytes 720928 | tf_op jit(solution)/shard_map/ppermute | solution.py:27
  265.5 5.1 %collective-permute-done.47 = bf16[2,2,2,64,704]{4,3,1,0,2:T(8,128)(2,1)S(1)} collective-permute-done((bf16[2,2,2,64,704]{4,3,1,0,2:T(8,128)(2,1)S(1)}, bf16[2,2,2,64,704]{4,3,1,0,2:T(8,128)(2,1)S(1)}, u32[]{:S(2)}, u32[]{:S(2)}) %collective-permute-start.47) | collective-permute-done | bytes 720928 | tf_op jit(solution)/shard_map/ppermute | solution.py:27
  274.3 4.0 collective-permute-done.46
  289.5 3.4 collective-permute-start.52
  299.2 5.3 %attention_backward_local.1 = (bf16[2,4,192,256]{3,2,1,0:T(8,128)(2,1)S(1)}, f32[4,192,256]{2,1,0:T(8,128)S(1)}) custom-call(bf16[4,192,256]{2,1,0:T(8,128)(2,1)S(1)} %bitcast.379, f32[4,192,256]{2,1,0:T(8,128)S(1)} %copy-done.9, bf16[4,192,256]{2,1,0:T(8,128)(2,1)S(1)} %bitcast.373, bf16[4,192,256]{2,1,0:T(8,128)(2,1)S(1)} %bitcast.375, ...), custom_call_target="tpu_custom_call" | custom-call | flops 3000000000 | bytes 5000000 | tf_op jit(solution)/shard_map/attention_backward_local/pallas_call | solution.py:485
  335.4 12.5 %attention_backward.1 = bf16[4,192,256]{2,1,0:T(8,128)(2,1)S(1)} custom-call(bf16[4,192,256]{2,1,0:T(8,128)(2,1)S(1)} %bitcast.380, f32[4,192,256]{2,1,0:T(8,128)S(1)} %copy-done.10, f32[4,192,256]{2,1,0:T(8,128)S(1)} %copy-done.17, f32[4,2,192,1]{3,2,1,0:T(8,128)S(1)} %copy-done.13, bf16[4,2,7,192,384]{4,3,2,1,0:T(8,128)(2,1)} %get-tuple-element.181.p_ref, ...), custom_call_target="tpu_custom_call" | custom-call | flops 16911433728 | bytes 20000000 | tf_op jit(solution)/shard_map/attention_backward/pallas_call | solution.py:507
  353.3 3.6 collective-permute-done.58
  362.2 3.8 multiply_reduce_fusion
  369.2 7.8 %collective-permute-done.66 = bf16[2,2,2,64,384]{4,3,1,0,2:T(8,128)(2,1)S(1)} collective-permute-done((bf16[2,2,2,64,384]{4,3,1,0,2:T(8,128)(2,1)S(1)}, bf16[2,2,2,64,384]{4,3,1,0,2:T(8,128)(2,1)S(1)}, u32[]{:S(2)}, u32[]{:S(2)}) %collective-permute-start.66) | collective-permute-done | bytes 393248 | tf_op jit(solution)/shard_map/ppermute | solution.py:27
  385.8 6.3 %collective-permute-done.69 = bf16[1,2,64,768]{3,2,1,0:T(8,128)(2,1)S(1)} collective-permute-done((bf16[1,2,64,768]{3,2,1,0:T(8,128)(2,1)S(1)}, bf16[1,2,64,768]{3,2,1,0:T(8,128)(2,1)S(1)}, u32[]{:S(2)}, u32[]{:S(2)}) %collective-permute-start.69) | collective-permute-done | bytes 196640 | tf_op jit(solution)/shard_map/ppermute | solution.py:27
  394.1 4.4 %collective-permute-done.70 = bf16[64,1152]{1,0:T(8,128)(2,1)S(1)} collective-permute-done((bf16[64,1152]{1,0:T(8,128)(2,1)S(1)}, bf16[64,1152]{1,0:T(8,128)(2,1)S(1)}, u32[]{:S(2)}, u32[]{:S(2)}) %collective-permute-start.70) | collective-permute-done | bytes 147488 | tf_op jit(solution)/shard_map/ppermute | solution.py:27
  403.9 7.8 %collective-permute-done.65 = bf16[192,1024]{1,0:T(8,128)(2,1)S(1)} collective-permute-done((bf16[192,1024]{1,0:T(8,128)(2,1)S(1)}, bf16[192,1024]{1,0:T(8,128)(2,1)S(1)}, u32[]{:S(2)}, u32[]{:S(2)}) %collective-permute-start.65) | collective-permute-done | bytes 393248 | tf_op jit(solution)/shard_map/ppermute | solution.py:27
  (545 shorter events, 226.7 us)
Async XLA Ops:
  16.4 17.2 %collective-permute-start.6 = (bf16[2,384,256]{2,1,0:T(8,128)(2,1)}, bf16[2,384,256]{2,1,0:T(8,128)(2,1)}, u32[]{:S(2)}, u32[]{:S(2)}) collective-permute-start(bf16[2,384,256]{2,1,0:T(8,128)(2,1)} %dynamic-slice_bitcast_fusion.6), channel_id=1, source_target_pairs={{0,8},{4,12},{8,0},{12,4},{16,24},{20,28},{24,16},{28,20},{1,9},{5... | collective-permute-start | bytes 1179656 | tf_op jit(solution)/shard_map/ppermute | solution.py:27
  17.1 18.5 %collective-permute-start.7 = (s32[192,128]{0,1:T(8,128)}, s32[192,128]{0,1:T(8,128)}, u32[]{:S(2)}, u32[]{:S(2)}) collective-permute-start(s32[192,128]{0,1:T(8,128)} %bitcast_add_fusion), channel_id=1, source_target_pairs={{0,8},{4,12},{8,0},{12,4},{16,24},{20,28},{24,16},{28,20},{1,9},{5... | collective-permute-start | bytes 294920 | tf_op jit(solution)/shard_map/ppermute | solution.py:27
  37.0 43.5 %collective-permute-start.11 = (bf16[2,384,256]{2,1,0:T(8,128)(2,1)S(1)}, bf16[2,384,256]{2,1,0:T(8,128)(2,1)S(1)}, u32[]{:S(2)}, u32[]{:S(2)}) collective-permute-start(bf16[2,384,256]{2,1,0:T(8,128)(2,1)S(1)} %get-tuple-element.110.refs_3_), channel_id=1, source_target_pairs={{0,16},{4,20},{8,24},{12,28},{1,17},{5,21},{9,25},{13,29},{2,18},{... | collective-permute-start | bytes 1179656 | tf_op jit(solution)/shard_map/ppermute | solution.py:692
  41.7 38.9 %collective-permute-start.12 = (bf16[2,384,256]{2,1,0:T(8,128)(2,1)S(1)}, bf16[2,384,256]{2,1,0:T(8,128)(2,1)S(1)}, u32[]{:S(2)}, u32[]{:S(2)}) collective-permute-start(bf16[2,384,256]{2,1,0:T(8,128)(2,1)S(1)} %get-tuple-element.110.refs_3_), channel_id=1, source_target_pairs={{0,4},{4,0},{8,12},{12,8},{16,20},{20,16},{24,28},{28,24},{1,5},{5... | collective-permute-start | bytes 1179656 | tf_op jit(solution)/shard_map/ppermute | solution.py:27
  43.2 35.1 %collective-permute-start.9 = (bf16[2,2,1,1,64,512]{5,4,1,0,3,2:T(8,128)(2,1)}, bf16[2,2,1,1,64,512]{5,4,1,0,3,2:T(8,128)(2,1)}, u32[]{:S(2)}, u32[]{:S(2)}) collective-permute-start(bf16[2,2,1,1,64,512]{5,4,1,0,3,2:T(8,128)(2,1)} %slice.246), channel_id=1, source_target_pairs={{0,4},{4,0},{8,12},{12,8},{16,20},{20,16},{24,28},{28,24},{1,5},{5... | collective-permute-start | bytes 786440 | tf_op jit(solution)/shard_map/ppermute | solution.py:27
  43.7 35.6 %collective-permute-start.10 = (bf16[2,2,1,1,64,640]{5,4,1,0,3,2:T(8,128)(2,1)}, bf16[2,2,1,1,64,640]{5,4,1,0,3,2:T(8,128)(2,1)}, u32[]{:S(2)}, u32[]{:S(2)}) collective-permute-start(bf16[2,2,1,1,64,640]{5,4,1,0,3,2:T(8,128)(2,1)} %slice.247), channel_id=1, source_target_pairs={{0,2},{1,3},{2,0},{3,1},{4,6},{5,7},{6,4},{7,5},{8,10},{9,11},{10,... | collective-permute-start | bytes 983048 | tf_op jit(solution)/shard_map/ppermute | solution.py:27
  50.3 30.3 %collective-permute-start.13 = (bf16[192,1024]{1,0:T(8,128)(2,1)}, bf16[192,1024]{1,0:T(8,128)(2,1)}, u32[]{:S(2)}, u32[]{:S(2)}) collective-permute-start(bf16[192,1024]{1,0:T(8,128)(2,1)} %slice_bitcast_fusion.2), channel_id=1, source_target_pairs={{0,8},{4,12},{8,0},{12,4},{16,24},{20,28},{24,16},{28,20},{1,9},{5... | collective-permute-start | bytes 1179656 | tf_op jit(solution)/shard_map/ppermute | solution.py:27
  80.6 26.5 %collective-permute-start.16 = (bf16[2,2,2,1,64,512]{5,4,1,0,3,2:T(8,128)(2,1)S(1)}, bf16[2,2,2,1,64,512]{5,4,1,0,3,2:T(8,128)(2,1)S(1)}, u32[]{:S(2)}, u32[]{:S(2)}) collective-permute-start(bf16[2,2,2,1,64,512]{5,4,1,0,3,2:T(8,128)(2,1)S(1)} %pad_maximum_fusion.28), channel_id=1, source_target_pairs={{0,2},{1,3},{2,0},{3,1},{4,6},{5,7},{6,4},{7,5},{8,10},{9,11},{10,... | collective-permute-start | bytes 1572872 | tf_op jit(solution)/shard_map/ppermute | solution.py:27
  81.2 27.2 %collective-permute-start.17 = (bf16[2,2,1,2,64,640]{5,4,1,0,3,2:T(8,128)(2,1)S(1)}, bf16[2,2,1,2,64,640]{5,4,1,0,3,2:T(8,128)(2,1)S(1)}, u32[]{:S(2)}, u32[]{:S(2)}) collective-permute-start(bf16[2,2,1,2,64,640]{5,4,1,0,3,2:T(8,128)(2,1)S(1)} %pad_maximum_fusion.27), channel_id=1, source_target_pairs={{0,4},{4,0},{8,12},{12,8},{16,20},{20,16},{24,28},{28,24},{1,5},{5... | collective-permute-start | bytes 1966088 | tf_op jit(solution)/shard_map/ppermute | solution.py:27
  82.6 26.0 %collective-permute-start.18 = (bf16[2,384,256]{2,1,0:T(8,128)(2,1)S(1)}, bf16[2,384,256]{2,1,0:T(8,128)(2,1)S(1)}, u32[]{:S(2)}, u32[]{:S(2)}) collective-permute-start(bf16[2,384,256]{2,1,0:T(8,128)(2,1)S(1)} %get-tuple-element.127.refs_7_), channel_id=1, source_target_pairs={{0,16},{4,20},{8,24},{12,28},{1,17},{5,21},{9,25},{13,29},{2,18},{... | collective-permute-start | bytes 1179656 | tf_op jit(solution)/shard_map/ppermute | solution.py:692
  141.7 32.9 %collective-permute-start.29 = (bf16[1024,256]{1,0:T(8,128)(2,1)S(1)}, bf16[1024,256]{1,0:T(8,128)(2,1)S(1)}, u32[]{:S(2)}, u32[]{:S(2)}) collective-permute-start(bf16[1024,256]{1,0:T(8,128)(2,1)S(1)} %copy-done.33), channel_id=1, source_target_pairs={{0,8},{4,12},{8,0},{12,4},{16,24},{20,28},{24,16},{28,20},{1,9},{5... | collective-permute-start | bytes 1572872 | tf_op jit(solution)/shard_map/ppermute | solution.py:27
  155.9 17.0 %collective-permute-start.30 = (bf16[2,2,1,1,64,704]{5,4,1,3,2,0:T(8,128)(2,1)S(1)}, bf16[2,2,1,1,64,704]{5,4,1,3,2,0:T(8,128)(2,1)S(1)}, u32[]{:S(2)}, u32[]{:S(2)}) collective-permute-start(bf16[2,2,1,1,64,704]{5,4,1,3,2,0:T(8,128)(2,1)S(1)} %pad_maximum_fusion.32), channel_id=1, source_target_pairs={{0,4},{4,0},{8,12},{12,8},{16,20},{20,16},{24,28},{28,24},{1,5},{5... | collective-permute-start | bytes 1081352 | tf_op jit(solution)/shard_map/ppermute | solution.py:27
  156.4 18.0 %collective-permute-start.31 = (bf16[2,2,1,1,64,704]{5,4,1,3,2,0:T(8,128)(2,1)S(1)}, bf16[2,2,1,1,64,704]{5,4,1,3,2,0:T(8,128)(2,1)S(1)}, u32[]{:S(2)}, u32[]{:S(2)}) collective-permute-start(bf16[2,2,1,1,64,704]{5,4,1,3,2,0:T(8,128)(2,1)S(1)} %pad_maximum_fusion.33), channel_id=1, source_target_pairs={{0,2},{1,3},{2,0},{3,1},{4,6},{5,7},{6,4},{7,5},{8,10},{9,11},{10,... | collective-permute-start | bytes 1081352 | tf_op jit(solution)/shard_map/ppermute | solution.py:27
  175.9 16.9 %collective-permute-start.34 = (bf16[768,256]{1,0:T(8,128)(2,1)S(1)}, bf16[768,256]{1,0:T(8,128)(2,1)S(1)}, u32[]{:S(2)}, u32[]{:S(2)}) collective-permute-start(bf16[768,256]{1,0:T(8,128)(2,1)S(1)} %bitcast.369), channel_id=1, source_target_pairs={{0,8},{4,12},{8,0},{12,4},{16,24},{20,28},{24,16},{28,20},{1,9},{5... | collective-permute-start | bytes 1179656 | tf_op jit(solution)/shard_map/ppermute | solution.py:27
  194.8 22.6 %collective-permute-start.33 = (bf16[192,1024]{1,0:T(8,128)(2,1)S(1)}, bf16[192,1024]{1,0:T(8,128)(2,1)S(1)}, u32[]{:S(2)}, u32[]{:S(2)}) collective-permute-start(bf16[192,1024]{1,0:T(8,128)(2,1)S(1)} %bitcast.448), channel_id=1, source_target_pairs={{0,1},{1,0},{2,3},{3,2},{4,5},{5,4},{6,7},{7,6},{8,9},{9,8},{10,11... | collective-permute-start | bytes 1179656 | tf_op jit(solution)/shard_map/ppermute | solution.py:27
  233.8 38.5 %collective-permute-start.43 = (bf16[2,192,1024]{2,1,0:T(8,128)(2,1)}, bf16[2,192,1024]{2,1,0:T(8,128)(2,1)}, u32[]{:S(2)}, u32[]{:S(2)}) collective-permute-start(bf16[2,192,1024]{2,1,0:T(8,128)(2,1)} %fusion.7), channel_id=1, source_target_pairs={{0,8},{4,12},{8,0},{12,4},{16,24},{20,28},{24,16},{28,20},{1,9},{5... | collective-permute-start | bytes 2359304 | tf_op jit(solution)/shard_map/ppermute | solution.py:27
  242.9 20.0 %collective-permute-start.45 = (bf16[2,2,2,64,704]{4,3,1,0,2:T(8,128)(2,1)}, bf16[2,2,2,64,704]{4,3,1,0,2:T(8,128)(2,1)}, u32[]{:S(2)}, u32[]{:S(2)}) collective-permute-start(bf16[2,2,2,64,704]{4,3,1,0,2:T(8,128)(2,1)} %bitcast.366), channel_id=1, source_target_pairs={{0,4},{4,0},{8,12},{12,8},{16,20},{20,16},{24,28},{28,24},{1,5},{5... | collective-permute-start | bytes 2162696 | tf_op jit(solution)/shard_map/ppermute | solution.py:27
  250.2 20.4 %collective-permute-start.47 = (bf16[2,2,2,64,704]{4,3,1,0,2:T(8,128)(2,1)S(1)}, bf16[2,2,2,64,704]{4,3,1,0,2:T(8,128)(2,1)S(1)}, u32[]{:S(2)}, u32[]{:S(2)}) collective-permute-start(bf16[2,2,2,64,704]{4,3,1,0,2:T(8,128)(2,1)S(1)} %bitcast.430), channel_id=1, source_target_pairs={{0,2},{1,3},{2,0},{3,1},{4,6},{5,7},{6,4},{7,5},{8,10},{9,11},{10,... | collective-permute-start | bytes 2162696 | tf_op jit(solution)/shard_map/ppermute | solution.py:27
  253.1 21.0 %collective-permute-start.49 = (bf16[2,192,1024]{2,1,0:T(8,128)(2,1)S(1)}, bf16[2,192,1024]{2,1,0:T(8,128)(2,1)S(1)}, u32[]{:S(2)}, u32[]{:S(2)}) collective-permute-start(bf16[2,192,1024]{2,1,0:T(8,128)(2,1)S(1)} %fusion.19), channel_id=1, source_target_pairs={{0,1},{1,0},{2,3},{3,2},{4,5},{5,4},{6,7},{7,6},{8,9},{9,8},{10,11... | collective-permute-start | bytes 2359304 | tf_op jit(solution)/shard_map/ppermute | solution.py:27
  288.8 17.5 %collective-permute-start.50 = (bf16[2,1,2,88,1024]{4,3,0,2,1:T(8,128)(2,1)}, bf16[2,1,2,88,1024]{4,3,0,2,1:T(8,128)(2,1)}, u32[]{:S(2)}, u32[]{:S(2)}) collective-permute-start(bf16[2,1,2,88,1024]{4,3,0,2,1:T(8,128)(2,1)} %bitcast.367), channel_id=1, source_target_pairs={{0,4},{4,0},{8,12},{12,8},{16,20},{20,16},{24,28},{28,24},{1,5},{5... | collective-permute-start | bytes 2162696 | tf_op jit(solution)/shard_map/ppermute | solution.py:27
  325.6 25.9 %collective-permute-start.55 = (bf16[2,2,2,64,512]{4,3,2,1,0:T(8,128)(2,1)S(1)}, bf16[2,2,2,64,512]{4,3,2,1,0:T(8,128)(2,1)S(1)}, u32[]{:S(2)}, u32[]{:S(2)}) collective-permute-start(bf16[2,2,2,64,512]{4,3,2,1,0:T(8,128)(2,1)S(1)} %dynamic-slice_bitcast_fusion), channel_id=1, source_target_pairs={{0,4},{4,0},{8,12},{12,8},{16,20},{20,16},{24,28},{28,24},{1,5},{5... | collective-permute-start | bytes 1572872 | tf_op jit(solution)/shard_map/ppermute | solution.py:27
  328.1 22.9 %collective-permute-start.57 = (bf16[2,2,2,64,256]{4,3,1,0,2:T(8,128)(2,1)S(1)}, bf16[2,2,2,64,256]{4,3,1,0,2:T(8,128)(2,1)S(1)}, u32[]{:S(2)}, u32[]{:S(2)}) collective-permute-start(bf16[2,2,2,64,256]{4,3,1,0,2:T(8,128)(2,1)S(1)} %bitcast.457), channel_id=1, source_target_pairs={{0,2},{1,3},{2,0},{3,1},{4,6},{5,7},{6,4},{7,5},{8,10},{9,11},{10,... | collective-permute-start | bytes 786440 | tf_op jit(solution)/shard_map/ppermute | solution.py:27
  329.4 20.0 %collective-permute-start.59 = (bf16[1,1,88,1024]{3,2,1,0:T(8,128)(2,1)S(1)}, bf16[1,1,88,1024]{3,2,1,0:T(8,128)(2,1)S(1)}, u32[]{:S(2)}, u32[]{:S(2)}) collective-permute-start(bf16[1,1,88,1024]{3,2,1,0:T(8,128)(2,1)S(1)} %constant_dynamic-slice_fusion.2), channel_id=1, source_target_pairs={{0,16},{4,20},{8,24},{12,28},{16,0},{20,4},{24,8},{28,12},{1,17},{... | collective-permute-start | bytes 540680 | tf_op jit(solution)/shard_map/ppermute | solution.py:27
  369.1 29.5 %collective-permute-start.64 = (bf16[2,192,1024]{2,1,0:T(8,128)(2,1)S(1)}, bf16[2,192,1024]{2,1,0:T(8,128)(2,1)}, u32[]{:S(2)}, u32[]{:S(2)}) collective-permute-start(bf16[2,192,1024]{2,1,0:T(8,128)(2,1)S(1)} %fusion.20), channel_id=1, source_target_pairs={{0,1},{1,0},{2,3},{3,2},{4,5},{5,4},{6,7},{7,6},{8,9},{9,8},{10,11... | collective-permute-start | bytes 2359304 | tf_op jit(solution)/shard_map/ppermute | solution.py:27
  (134 other events, 1047.4 us)
